TPU v7x, 512 devices: a whole 4x8x8 slice. The times are simulated.
512 devices in a mesh: region: 8 (over y), super: 64 (over x, z, core).
Axes of the slice: x: 4, y: 8, z: 8, core: 2. Of those that a mesh axis runs over, the one named last changes fastest.
Arguments:
- obs_coords: float32 [2, 2097152], P(None, ('region', 'super')), may hold values from 0 to 1, as said below
- obs_values: bfloat16 [64, 2097152], P(None, ('region', 'super')), may hold values from -6 to 6
- obs_precision: float32 [2097152], P(('region', 'super')), may hold values from 0.0009765625 to 0.009765625
- site_coords: float32 [2, 262144], P(None, ('region', 'super')), may hold values from 0 to 1, as said below
- length_scale: float32 [3], replicated, may hold values from 0.0005859375 to 0.3, as said below
- global_knots: float32 [2, 256], replicated, may hold values from 0 to 1
- region_knots: float32 [64, 2, 256], P('super'), may hold values from 0 to 1, as said below
- leaf_knots: float32 [512, 2, 256], P(('region', 'super')), may hold values from 0 to 1, as said below
- global_prior: float32 [256, 256], replicated, as said below
- region_prior: float32 [64, 256, 256], P('super'), as said below
- leaf_prior: float32 [512, 256, 256], P(('region', 'super')), as said below
Outputs:
- prediction: float32 [64, 262144], P(None, ('region', 'super'))
Inputs may be any that keep to these rules, and one draw needn't show every extreme that they name: `global_prior`: symmetric; each diagonal entry exceeds the sum of magnitudes of the other entries of its row. `region_prior`: each region's matrix symmetric; each diagonal entry exceeds the sum of magnitudes of the other entries of its row. `leaf_prior`: each leaf's matrix symmetric; each diagonal entry exceeds the sum of magnitudes of the other entries of its row. `obs_coords`: the region cells tile the unit square as a grid, each split into a grid of leaf cells; leaf l's observations lie inside leaf l's cell. `site_coords`: leaf l's sites lie inside leaf l's cell. `region_knots`: region g's knots lie inside region g's cell. `leaf_knots`: leaf l's knots lie inside leaf l's cell. `length_scale`: the global scale lies in 0.15 to 0.3, the regional scale in 0.7 to 1.0 times 1 / sqrt(16384), the leaf scale in 0.3 to 0.9 times 1 / sqrt(512).
All inputs are finite; a program needn't handle non-finite values.
Results may differ from a plain program's by a relative error of at most 0.0003.
The roundings to bfloat16 on the way count: a program that leaves them out, or rounds other values in their place, can miss the bound.
Values sent between devices are 32-bit elements; how exact they have to be, the bound alone decides.
A program may use at most 64 MiB of HBM per device.

v0:
```python
import jax
import jax.numpy as jnp
from jax import lax
from jax.sharding import Mesh
from jax.sharding import PartitionSpec as P

R = 256
REGION_SUPER = ("region", "super_0", "super_1", "super_2")
SUPER = ("super_0", "super_1", "super_2")


HIGH = lax.Precision.HIGHEST


def copy_for_each(x, axis):
    copies = jnp.broadcast_to(x, (lax.axis_size(axis), *x.shape))
    return lax.all_to_all(copies, axis, split_axis=0, concat_axis=0, tiled=True)


def of_everyone(x, axis):
    return copy_for_each(x, axis).sum(axis=0)


def in_blocks(x, dim, peers):
    dims = x.shape
    tiles = x.reshape(*dims[:dim], peers, dims[dim] // peers, *dims[dim + 1 :])
    return jnp.moveaxis(tiles, dim, 0)


def summed_on_arrival(x, axis, dim):
    peers = lax.axis_size(axis)
    tiles = lax.all_to_all(in_blocks(x, dim, peers), axis, 0, 0, tiled=True)
    return jnp.sum(tiles, axis=0)


def sum_in_two_steps(x, axes, dim):
    far, near = axes
    tiles = in_blocks(x, dim, lax.axis_size(far))
    nearer = summed_on_arrival(tiles, near, dim + 1)
    arrived = lax.all_to_all(nearer, far, split_axis=0, concat_axis=0, tiled=True)
    return arrived.sum(axis=0)


def rows_for(lines, peers):
    spare = -lines.shape[0] % peers
    if not spare:
        return lines
    return jnp.concatenate([lines, jnp.zeros((spare, *lines.shape[1:]), lines.dtype)])


def joined_along(tiles, dim):
    dims = list(tiles.shape[1:])
    dims[dim] *= tiles.shape[0]
    return jnp.moveaxis(tiles, 0, dim).reshape(dims)


def gather_axes(x, axes, dim):
    far, near = axes
    tiles = copy_for_each(copy_for_each(x, far), near)
    return joined_along(tiles.swapaxes(0, 1).reshape(-1, *x.shape), dim)


def nested_sum(x, axes):
    lines = x.reshape(-1)
    own = sum_in_two_steps(
        rows_for(lines, lax.axis_size(axes[0]) * lax.axis_size(axes[1])), axes, 0
    )
    whole = gather_axes(own, axes, 0)
    return whole[: len(lines)].reshape(x.shape)


def basis_rows(coords, knots, scale):
    diff_x = coords[0][:, None] - knots[0][None, :]
    diff_y = coords[1][:, None] - knots[1][None, :]
    return jnp.exp(-0.5 * (diff_x * diff_x + diff_y * diff_y) / (scale * scale))


def basis_cols(knots, coords, scale):
    diff_x = knots[0][:, None] - coords[0][None, :]
    diff_y = knots[1][:, None] - coords[1][None, :]
    return jnp.exp(-0.5 * (diff_x * diff_x + diff_y * diff_y) / (scale * scale))


def leaf_terms(coords, values, precision, knots_g, knots_r, knots_l, scales, prior_l):
    weight = jnp.sqrt(precision)[:, None]
    stacked = jnp.concatenate(
        [
            basis_rows(coords, knots_g, scales[0]),
            basis_rows(coords, knots_r, scales[1]),
            basis_rows(coords, knots_l, scales[2]),
            values.astype(jnp.float32).T,
        ],
        axis=1,
    )
    scaled = (stacked * weight).astype(jnp.bfloat16)
    gram = lax.dot_general(
        scaled, scaled, (((0,), (0,)), ((), ())), preferred_element_type=jnp.float32
    )
    cross = gram[2 * R : 3 * R, : 2 * R]
    factor = jnp.linalg.cholesky(prior_l + gram[2 * R : 3 * R, 2 * R : 3 * R])
    rhs = jnp.concatenate([cross, gram[2 * R : 3 * R, 3 * R :]], axis=1)
    solved = jax.scipy.linalg.cho_solve((factor, True), rhs)
    left = jnp.concatenate([gram[: 2 * R, : 2 * R], gram[: 2 * R, 3 * R :]], axis=1)
    schur = left - jnp.dot(cross.T, solved, precision=HIGH)
    return (schur, solved)


def region_terms(rows, prior_r):
    factor = jnp.linalg.cholesky(prior_r + rows[:, R : 2 * R])
    rhs = jnp.concatenate([rows[:, :R], rows[:, 2 * R :]], axis=1)
    solved = jax.scipy.linalg.cho_solve((factor, True), rhs)
    correction = jnp.dot(rows[:, :R].T, solved, precision=HIGH)
    return (solved, correction)


def global_part(schur):
    return jnp.concatenate([schur[:R, :R], schur[:R, 2 * R :]], axis=1)


def shards(
    obs_coords,
    obs_values,
    obs_precision,
    site_coords,
    length_scale,
    global_knots,
    region_knots,
    leaf_knots,
    global_prior,
    region_prior,
    leaf_prior,
):
    schur, solved = leaf_terms(
        obs_coords,
        obs_values,
        obs_precision,
        global_knots,
        region_knots[0],
        leaf_knots[0],
        length_scale,
        leaf_prior[0],
    )
    rows = of_everyone(schur[R : 2 * R], "region")
    region_solved, correction = region_terms(rows, region_prior[0])
    share = global_part(schur) - correction / lax.axis_size("region")
    upper = nested_sum(share, ("region", ("super_0", "super_1", "super_2")))
    factor = jnp.linalg.cholesky(global_prior + upper[:, :R])
    global_weights = jax.scipy.linalg.cho_solve((factor, True), upper[:, R:])
    region_weights = region_solved[:, R:] - jnp.dot(
        region_solved[:, :R], global_weights, precision=HIGH
    )
    upper_weights = jnp.concatenate([global_weights, region_weights], axis=0)
    leaf_weights = solved[:, 2 * R :] - jnp.dot(solved[:, : 2 * R], upper_weights, precision=HIGH)
    weights = jnp.concatenate([upper_weights, leaf_weights], axis=0)
    table = jnp.concatenate(
        [
            basis_cols(global_knots, site_coords, length_scale[0]),
            basis_cols(region_knots[0], site_coords, length_scale[1]),
            basis_cols(leaf_knots[0], site_coords, length_scale[2]),
        ],
        axis=0,
    )
    return jnp.dot(weights.T, table, precision=HIGH)


def solution(mesh):
    split = Mesh(
        mesh.devices.reshape(mesh.shape["region"], 4, 8, 2),
        ("region", "super_0", "super_1", "super_2"),
    )
    return jax.shard_map(
        shards,
        mesh=split,
        in_specs=(
            P(None, REGION_SUPER),
            P(None, REGION_SUPER),
            P(REGION_SUPER),
            P(None, REGION_SUPER),
            P(),
            P(),
            P(SUPER, None, None),
            P(REGION_SUPER, None, None),
            P(),
            P(SUPER, None, None),
            P(REGION_SUPER, None, None),
        ),
        out_specs=P(None, REGION_SUPER),
        check_vma=False,
    )
```

profile of v0, /device:TPU:1, one launch (start us, length us, event | category | flops | bytes accessed | tf_op | source)
XLA Modules:
  0.0 418.9 jit_solution(17604024180645550257)
XLA Ops:
  11.5 4.0 divide_exponential_fusion.2
  15.6 8.0 %fusion.1 = f32[832,832]{0,1:T(8,128)S(1)} fusion(f32[4096,64]{1,0:T(8,128)S(1)} %copy-done.1, f32[4096,256]{1,0:T(8,128)S(1)} %get-tuple-element.76, f32[4096,256]{1,0:T(8,128)S(1)} %get-tuple-element.75, f32[4096,256]{1,0:T(8,128)S(1)} %get-tuple-element.74, f32[4096]{0:T(1024)S(1)} %sqrt.3), kind=kOutput, calls=%fused_computation.8 | convolution fusion | flops 5687738368 | bytes 16416768 | tf_op jit(solution)/shard_map/dot_general | solution.py:96
  26.5 11.7 %cholesky.172 = f32[128,128]{1,0:T(8,128)S(1)} custom-call(f32[128,128]{1,0:T(8,128)S(1)} %cholesky.270), custom_call_target="Cholesky" | custom-call | tf_op jit(solution)/shard_map/jit(cholesky)/cholesky | solution.py:100
  38.2 10.2 %custom-call.34 = f32[1,128,128]{1,2,0:T(8,128)S(1)} custom-call(f32[1,128,128]{2,1,0:T(8,128)S(1)} %get-tuple-element.73), custom_call_target="InvertDiagBlocksLowerTriangular" | custom-call | tf_op jit(solution)/shard_map/jit(cholesky)/cholesky | solution.py:100
  48.9 11.7 %cholesky.189 = f32[128,128]{1,0:T(8,128)S(1)} custom-call(f32[128,128]{1,0:T(8,128)S(1)} %convolution_subtract_fusion.8), custom_call_target="Cholesky" | custom-call | tf_op jit(solution)/shard_map/jit(cholesky)/cholesky | solution.py:100
  62.7 3.9 while.3
  66.7 19.7 %custom-call.29 = f32[2,128,128]{1,2,0:T(8,128)S(1)} custom-call(f32[2,128,128]{2,1,0:T(8,128)S(1)} %get-tuple-element.13), custom_call_target="InvertDiagBlocksLowerTriangular" | custom-call | tf_op jit(solution)/shard_map/jit(_cho_solve)/triangular_solve | solution.py:102
  93.6 8.0 %all-to-all-start = ((f32[8,256,576]{1,2,0:T(8,128)}), f32[8,256,576]{1,2,0:T(8,128)}, u32[]{:S(2)}, u32[]{:S(2)}) async-start(f32[8,256,576]{1,2,0:T(8,128)} %broadcast_in_dim.11), calls=%async_computation | async-start | bytes 9437184 | tf_op jit(solution)/shard_map/all_to_all | solution.py:17
  101.8 103.2 %all-to-all-done = f32[8,256,576]{1,2,0:T(8,128)} async-done(((f32[8,256,576]{1,2,0:T(8,128)}), f32[8,256,576]{1,2,0:T(8,128)}, u32[]{:S(2)}, u32[]{:S(2)}) %all-to-all-start) | async-done | bytes 4718624 | tf_op jit(solution)/shard_map/all_to_all | solution.py:17
  208.0 11.7 %cholesky.206 = f32[128,128]{1,0:T(8,128)S(1)} custom-call(f32[128,128]{1,0:T(8,128)S(1)} %cholesky.273), custom_call_target="Cholesky" | custom-call | tf_op jit(solution)/shard_map/jit(cholesky)/cholesky | solution.py:109
  219.8 9.8 %custom-call.35 = f32[1,128,128]{1,2,0:T(8,128)S(1)} custom-call(f32[1,128,128]{2,1,0:T(8,128)S(1)} %get-tuple-element.69), custom_call_target="InvertDiagBlocksLowerTriangular" | custom-call | tf_op jit(solution)/shard_map/jit(cholesky)/cholesky | solution.py:109
  230.1 11.7 %cholesky.223 = f32[128,128]{1,0:T(8,128)S(1)} custom-call(f32[128,128]{1,0:T(8,128)S(1)} %convolution_subtract_fusion.7), custom_call_target="Cholesky" | custom-call | tf_op jit(solution)/shard_map/jit(cholesky)/cholesky | solution.py:109
  244.5 4.1 while.4
  248.6 19.9 %custom-call.30 = f32[2,128,128]{1,2,0:T(8,128)S(1)} custom-call(f32[2,128,128]{2,1,0:T(8,128)S(1)} %get-tuple-element.21), custom_call_target="InvertDiagBlocksLowerTriangular" | custom-call | tf_op jit(solution)/shard_map/jit(_cho_solve)/triangular_solve | solution.py:111
  271.4 35.6 %all_to_all.34 = f32[64,8,160]{2,1,0:T(8,128)S(1)} all-to-all(f32[64,8,160]{2,1,0:T(8,128)S(1)} %copy.36), channel_id=1, replica_groups=mesh['region'=8,'super_0'=4,'super_1'=8,'super_2'=2] {'super_0','super_1..., dimensions={0} | all-to-all | bytes 655360 | tf_op jit(solution)/shard_map/all_to_all | solution.py:32
  307.1 8.9 %all_to_all.35 = f32[8,1,160]{2,1,0:T(1,128)S(1)} all-to-all(f32[8,1,160]{2,1,0:T(1,128)S(1)} %all_to_all.23), channel_id=1, replica_groups=mesh['region'=8,'super_0'=4,'super_1'=8,'super_2'=2] {'region'}, dimensions={0} | all-to-all | bytes 10240 | tf_op jit(solution)/shard_map/all_to_all | solution.py:40
  316.1 8.9 %all_to_all.33 = f32[8,1,160]{2,1,0:T(1,128)S(1)} all-to-all(f32[8,1,160]{2,1,0:T(1,128)S(1)} %broadcast_in_dim.12), channel_id=1, replica_groups=mesh['region'=8,'super_0'=4,'super_1'=8,'super_2'=2] {'region'}, dimensions={0} | all-to-all | bytes 10240 | tf_op jit(solution)/shard_map/all_to_all | solution.py:17
  325.8 8.9 %all-to-all-start.4 = ((f32[64,8,160]{2,1,0:T(8,128)}), f32[64,8,160]{2,1,0:T(8,128)S(1)}, u32[]{:S(2)}, u32[]{:S(2)}) async-start(f32[64,8,160]{2,1,0:T(8,128)} %broadcast_in_dim.13), calls=%async_computation.4 | async-start | bytes 1048576 | tf_op jit(solution)/shard_map/all_to_all | solution.py:17
  336.2 15.8 %all-to-all-done.4 = f32[64,8,160]{2,1,0:T(8,128)S(1)} async-done(((f32[64,8,160]{2,1,0:T(8,128)}), f32[64,8,160]{2,1,0:T(8,128)S(1)}, u32[]{:S(2)}, u32[]{:S(2)}) %all-to-all-start.4) | async-done | bytes 327712 | tf_op jit(solution)/shard_map/all_to_all | solution.py:17
  352.7 11.7 %cholesky.240 = f32[128,128]{1,0:T(8,128)S(1)} custom-call(f32[128,128]{1,0:T(8,128)S(1)} %cholesky.276), custom_call_target="Cholesky" | custom-call | tf_op jit(solution)/shard_map/jit(cholesky)/cholesky | solution.py:147
  364.5 9.8 %custom-call.36 = f32[1,128,128]{1,2,0:T(8,128)S(1)} custom-call(f32[1,128,128]{2,1,0:T(8,128)S(1)} %get-tuple-element.65), custom_call_target="InvertDiagBlocksLowerTriangular" | custom-call | tf_op jit(solution)/shard_map/jit(cholesky)/cholesky | solution.py:147
  374.8 11.7 %cholesky.257 = f32[128,128]{1,0:T(8,128)S(1)} custom-call(f32[128,128]{1,0:T(8,128)S(1)} %convolution_subtract_fusion.6), custom_call_target="Cholesky" | custom-call | tf_op jit(solution)/shard_map/jit(cholesky)/cholesky | solution.py:147
  389.3 4.1 while.5
  393.4 20.0 %custom-call.31 = f32[2,128,128]{1,2,0:T(8,128)S(1)} custom-call(f32[2,128,128]{2,1,0:T(8,128)S(1)} %get-tuple-element.29), custom_call_target="InvertDiagBlocksLowerTriangular" | custom-call | tf_op jit(solution)/shard_map/jit(_cho_solve)/triangular_solve | solution.py:148
  (133 shorter events, 48.9 us)
Async XLA Ops:
  0.0 11.5 %copy-start.5 = (f32[4096]{0:T(1024)S(1)}, f32[4096]{0:T(1024)}, u32[]{:S(2)}) copy-start(f32[4096]{0:T(1024)} %param.14) | copy-start | bytes 49156
  11.5 4.1 copy-start.1
  15.5 9.6 %copy-start.2 = (f32[1,256,256]{2,1,0:T(8,128)S(1)}, f32[1,256,256]{2,1,0:T(8,128)}, u32[]{:S(2)}) copy-start(f32[1,256,256]{2,1,0:T(8,128)} %param.22) | copy-start | bytes 786436
  23.5 1.6 copy-start
  93.6 8.1 %copy-start.3 = (f32[1,256,256]{2,1,0:T(8,128)S(1)}, f32[1,256,256]{2,1,0:T(8,128)}, u32[]{:S(2)}) copy-start(f32[1,256,256]{2,1,0:T(8,128)} %param.21) | copy-start | bytes 786436
  93.6 111.4 %all-to-all-start = ((f32[8,256,576]{1,2,0:T(8,128)}), f32[8,256,576]{1,2,0:T(8,128)}, u32[]{:S(2)}, u32[]{:S(2)}) async-start(f32[8,256,576]{1,2,0:T(8,128)} %broadcast_in_dim.11), calls=%async_computation | async-start | bytes 9437184 | tf_op jit(solution)/shard_map/all_to_all | solution.py:17
  269.4 65.4 %copy-start.4 = (f32[256,256]{1,0:T(8,128)S(1)}, f32[256,256]{1,0:T(8,128)}, u32[]{:S(2)}) copy-start(f32[256,256]{1,0:T(8,128)} %param.20) | copy-start | bytes 786436
  269.7 65.3 %copy-start.6 = (f32[2,512]{1,0:T(2,128)S(1)}, f32[2,512]{1,0:T(2,128)}, u32[]{:S(2)}) copy-start(f32[2,512]{1,0:T(2,128)} %param.15) | copy-start | bytes 12292
  325.8 26.1 %all-to-all-start.4 = ((f32[64,8,160]{2,1,0:T(8,128)}), f32[64,8,160]{2,1,0:T(8,128)S(1)}, u32[]{:S(2)}, u32[]{:S(2)}) async-start(f32[64,8,160]{2,1,0:T(8,128)} %broadcast_in_dim.13), calls=%async_computation.4 | async-start | bytes 1048576 | tf_op jit(solution)/shard_map/all_to_all | solution.py:17
where the time goes:
time: 422 us; the launch traced here: 419 us
  other arithmetic  174 us (41%)
  waiting for transfers between devices  119 us (28%)
  blocking collectives  53.5 us (13%)
  local copies, waits for them, and re-layouts  25.7 us (6%)
  matrix products  21 us (5%)
  starting transfers between devices  17 us (4%)
  between operations  8.84 us (2%)
    all_to_all x2, waiting for transfers between devices, copy_for_each(): return lax.all_to_all(copies, axis, split_axis=0, concat_axis=0, tiled=True)  119 us
    all_to_all x1, blocking collectives, summed_on_arrival(): tiles = lax.all_to_all(in_blocks(x, dim, peers), axis, 0, 0, tiled=True)  35.6 us
    another operation x7, other arithmetic, shards(): factor = jnp.linalg.cholesky(global_prior + upper[:, :R])  34.7 us
    another operation x7, other arithmetic, region_terms(): factor = jnp.linalg.cholesky(prior_r + rows[:, R:2 * R])  34.7 us
    another operation x6, other arithmetic, leaf_terms(): factor = jnp.linalg.cholesky(prior_l + gram[2 * R:3 * R, 2 * R:3 * R])  34.4 us
    another operation x2, other arithmetic, shards(): global_weights = jax.scipy.linalg.cho_solve((factor, True), upper[:, R:])  20 us
    another operation x2, other arithmetic, region_terms(): solved = jax.scipy.linalg.cho_solve((factor, True), rhs)  19.9 us
    another operation x3, other arithmetic, leaf_terms(): solved = jax.scipy.linalg.cho_solve((factor, True), rhs)  19.7 us
  transfers between devices with their start and end apart: 2, of which 2 were waited for; matrix products, arithmetic and copies ran while one was open for 0% of the time, Pallas kernels for 0%

commit v1 on v0

v1 whole, which is shorter than its diff:
```python
import functools

import jax
import jax.numpy as jnp
from jax import lax
from jax.experimental import pallas as pl
from jax.experimental.pallas import tpu as pltpu
from jax.sharding import Mesh
from jax.sharding import PartitionSpec as P

R = 256
B = 8
H = 128
FIELDS = 64
F32 = jnp.float32
BF16 = jnp.bfloat16
HIGH = lax.Precision.HIGHEST
MESH = pl.DeviceIdType.MESH
REGION_SUPER = ("region", "super_0", "super_1", "super_2")
SUPER = ("super_0", "super_1", "super_2")
VMEM = pl.BlockSpec(memory_space=pltpu.VMEM)
SMEM = pl.BlockSpec(memory_space=pltpu.SMEM)
LIMIT = 40 * 1024 * 1024


def parts_of(x):
    high = x.astype(BF16).astype(F32)
    rest = x - high
    middle = rest.astype(BF16).astype(F32)
    return high, middle, rest - middle


def left_stack(x):
    h, m, l = parts_of(x)
    return jnp.concatenate([h, h, m, h, l, m], axis=0).astype(BF16)


def right_stack(x):
    h, m, l = parts_of(x)
    return jnp.concatenate([h, m, h, l, h, m], axis=0).astype(BF16)


def total_of(terms):
    terms = list(terms)
    while len(terms) > 1:
        pairs = [terms[i] + terms[i + 1] for i in range(0, len(terms) - 1, 2)]
        terms = pairs + terms[len(pairs) * 2 :]
    return terms[0]


def columns_of(x, first):
    zero = jnp.zeros((B, H), jnp.int32)
    return [jnp.take_along_axis(x, zero + (first + j), axis=1) for j in range(B)]


def row_of(ref, r):
    return jnp.broadcast_to(ref[r : r + 1, :], (B, ref.shape[1]))


def twice(x):
    return jnp.concatenate([x, x], axis=1)


def eliminate(f_ref, w_ref, v_ref, cols_ref, rows_ref, lh_ref, xh_ref, between=None):
    lane = lax.broadcasted_iota(jnp.int32, (B, R), 1)
    sub = lax.broadcasted_iota(jnp.int32, (B, R), 0)
    sub_half = lax.broadcasted_iota(jnp.int32, (B, H), 0)
    lane_all = lax.broadcasted_iota(jnp.int32, (R, R), 1)
    lh_ref[...] = jnp.zeros_like(lh_ref)
    xh_ref[...] = jnp.zeros_like(xh_ref)

    def body(k, panel):
        base = pl.multiple_of(k * B, B)
        half = lax.div(k, 16)
        at = (k - 16 * half) * B
        diag = jnp.where(half == 0, panel[:, :H], panel[:, H:])
        for j, column in enumerate(columns_of(diag, at)):
            cols_ref[j * B : (j + 1) * B, :] = column
        mark = (lane >= base) & (lane < base + B)
        eye = jnp.where(lane == base + sub, 1.0, 0.0).astype(F32)
        rows_ref[...] = jnp.where(mark, eye, panel)
        update = lax.dot_general(
            lh_ref[...], xh_ref[...], (((0,), (0,)), ((), ())), preferred_element_type=F32
        )
        last = (lane_all >= base - B) & (lane_all < base)
        f_ref[...] = jnp.where(last, 0.0, f_ref[...]) - update
        s = {}
        for j in range(B):
            for i in range(j + 1):
                s[i, j] = row_of(cols_ref, j * B + i)
        low = {}
        inv = []
        for p in range(B):
            inv.append(1.0 / s[p, p])
            for i in range(p + 1, B):
                m = s[p, i] * inv[p]
                for j in range(i, B):
                    s[i, j] = s[i, j] - m * s[p, j]
                for c in range(p):
                    low[i, c] = low[i, c] - m * low[p, c]
                low[i, p] = -m
        following = pl.multiple_of(jnp.minimum(k + 1, R // B - 1) * B, B)
        ahead = f_ref[pl.ds(following, B), :]
        g = columns_of(jnp.where(half == 0, ahead[:, :H], ahead[:, H:]), at)
        rows = [row_of(rows_ref, j) for j in range(B)]
        row = [total_of([twice(low[j, m]) * rows[m] for m in range(j)] + [rows[j]]) for j in range(B)]
        lcol = [total_of([g[m] * low[j, m] for m in range(j)] + [g[j]]) * inv[j] for j in range(B)]
        panel_next = jnp.where(mark, 0.0, ahead) - total_of(
            [twice(lcol[j]) * row[j] for j in range(B)]
        )
        dcol = inv[0]
        mine = row[0]
        for i in range(1, B):
            dcol = jnp.where(sub_half == i, inv[i], dcol)
            mine = jnp.where(sub == i, row[i], mine)
        x = twice(dcol) * mine
        done = lane < base + B
        w_ref[pl.ds(base, B), :] = jnp.where(done, mine, 0.0)
        v_ref[pl.ds(base, B), :] = jnp.where(done, x, 0.0)
        lh_ref[...] = left_stack(jnp.where(done, 0.0, mine))
        xh_ref[...] = right_stack(x)
        return panel_next

    if between is None:
        lax.fori_loop(0, R // B, body, f_ref[0:B, :])
    else:
        panel = lax.fori_loop(0, R // B // 2, body, f_ref[0:B, :])
        between()
        lax.fori_loop(R // B // 2, R // B, body, panel)


def eliminate_scratch():
    return [
        pltpu.VMEM((R, R), F32),
        pltpu.VMEM((B * B, H), F32),
        pltpu.VMEM((B, R), F32),
        pltpu.VMEM((48, R), BF16),
        pltpu.VMEM((48, R), BF16),
    ]


def dot(a, b):
    return jnp.dot(a, b, precision=HIGH, preferred_element_type=F32)


def dot_t(a, b):
    return lax.dot_general(a, b, (((0,), (0,)), ((), ())), precision=HIGH, preferred_element_type=F32)


def gram_of(a, b):
    return lax.dot_general(a, b, (((1,), (1,)), ((), ())), preferred_element_type=F32)


def upright(knots):
    spare = jnp.zeros((6, R), F32)
    return jnp.concatenate([knots, spare], axis=0).T


def basis(knots, places, scale):
    diff_x = knots[:, 0:1] - places[0:1, :]
    diff_y = knots[:, 1:2] - places[1:2, :]
    return jnp.exp((diff_x * diff_x + diff_y * diff_y) * scale)


def factors(scale_ref):
    return [-0.5 / (scale_ref[i] * scale_ref[i]) for i in range(3)]


CHUNK = 512


def leaf_kernel(
    scale_ref, gk_hbm, rk_hbm, lk_hbm, coords_hbm, precision_hbm, values_hbm, sites_hbm, prior_hbm,
    mc_ref, gs_ref, t2_ref, w_ref, table_ref,
    gk_ref, rk_ref, lk_ref, coords_ref, precision_ref, values_ref, sites_ref, prior_ref, sems,
    z_ref, gv_ref, gr_ref, gg_ref, v_ref, f_ref, *scratch,
):
    sources = (gk_hbm, rk_hbm, lk_hbm, coords_hbm, precision_hbm, values_hbm, sites_hbm, prior_hbm)
    targets = (gk_ref, rk_ref, lk_ref, coords_ref, precision_ref, values_ref, sites_ref, prior_ref)
    copies = [pltpu.make_async_copy(a, b, sems.at[n]) for n, (a, b) in enumerate(zip(sources, targets))]
    for copy in copies:
        copy.start()
    for copy in copies[:6]:
        copy.wait()
    scale = factors(scale_ref)
    knots = [upright(lk_ref[...]), upright(rk_ref[...]), upright(gk_ref[...])]
    scales = [scale[2], scale[1], scale[0]]
    gv_ref[...] = jnp.zeros_like(gv_ref)
    gr_ref[...] = jnp.zeros_like(gr_ref)
    gg_ref[...] = jnp.zeros_like(gg_ref)

    def step(i, _):
        at = pl.ds(pl.multiple_of(i * CHUNK, CHUNK), CHUNK)
        places = coords_ref[:, at]
        weight = jnp.sqrt(precision_ref[:, at])
        for n in range(3):
            z_ref[n * R : (n + 1) * R, :] = (basis(knots[n], places, scales[n]) * weight).astype(BF16)
        z_ref[3 * R :, :] = (values_ref[:, at].astype(F32) * weight).astype(BF16)
        gv_ref[...] += gram_of(z_ref[:R, :], z_ref[...])
        gr_ref[...] += gram_of(z_ref[R : 2 * R, :], z_ref[R:, :])
        gg_ref[...] += gram_of(z_ref[2 * R : 3 * R, :], z_ref[2 * R :, :])
        return 0

    lax.fori_loop(0, coords_ref.shape[1] // CHUNK, step, 0)
    for copy in copies[6:]:
        copy.wait()
    for n, (k, s) in enumerate(zip(knots[::-1], scales[::-1])):
        order = n
        table_ref[order * R : (order + 1) * R, :] = basis(k, sites_ref[...], s)
    f_ref[...] = prior_ref[...] + gv_ref[:, :R]
    eliminate(f_ref, w_ref, v_ref, *scratch)
    t1 = dot(w_ref[...], gv_ref[:, R:])
    t2 = dot(v_ref[...], gv_ref[:, R:])
    t2_ref[...] = t2
    regional = gr_ref[...] - dot_t(t1[:, :R], t2)
    upper = gg_ref[...] - dot_t(t1[:, R : 2 * R], t2[:, R:])
    mc_ref[0:H, :] = regional[:H, :H]
    mc_ref[H : 2 * H, :] = regional[H:, :H]
    mc_ref[2 * H : 3 * H, :] = regional[H:, H:R]
    for r in range(2):
        for c in range(2):
            n = 3 + 2 * r + c
            mc_ref[n * H : (n + 1) * H, :] = regional[r * H : (r + 1) * H, R + c * H : R + (c + 1) * H]
    mc_ref[7 * H :, :] = jnp.concatenate([regional[:H, 2 * R :], regional[H:, 2 * R :]], axis=1)
    pack_global(gs_ref, upper)


def pack_global(out_ref, upper):
    out_ref[0:H, :] = upper[:H, :H]
    out_ref[H : 2 * H, :] = upper[H:, :H]
    out_ref[2 * H : 3 * H, :] = upper[H:, H:R]
    out_ref[3 * H :, :] = jnp.concatenate([upper[:H, R:], upper[H:, R:]], axis=1)


def whole_of(ref, first):
    a, b, c = (ref[(first + n) * H : (first + n + 1) * H, :] for n in range(3))
    return jnp.concatenate(
        [jnp.concatenate([a, b.T], axis=1), jnp.concatenate([b, c], axis=1)], axis=0
    )


def fields_of(ref, block):
    y = ref[block * H : (block + 1) * H, :]
    return jnp.concatenate([y[:, :FIELDS], y[:, FIELDS:]], axis=0)


def shape(*dims):
    return jax.ShapeDtypeStruct(dims, F32)


def leaf(scales, coords, values, precision, gk, rk, lk, prior, sites):
    operands = (gk, rk, lk, coords, precision, values, sites, prior)
    return pl.pallas_call(
        leaf_kernel,
        name="leaf",
        out_shape=[
            shape(8 * H, H), shape(4 * H, H), shape(R, 2 * R + FIELDS), shape(R, R),
            shape(3 * R, sites.shape[1]),
        ],
        in_specs=[SMEM] + [pl.BlockSpec(memory_space=pl.ANY)] * 8,
        out_specs=[VMEM] * 5,
        scratch_shapes=[pltpu.VMEM(a.shape, a.dtype) for a in operands]
        + [pltpu.SemaphoreType.DMA((8,))]
        + [
            pltpu.VMEM((3 * R + FIELDS, CHUNK), BF16),
            pltpu.VMEM((R, 3 * R + FIELDS), F32),
            pltpu.VMEM((R, 2 * R + FIELDS), F32),
            pltpu.VMEM((R, R + FIELDS), F32),
            pltpu.VMEM((R, R), F32),
        ] + eliminate_scratch(),
        compiler_params=pltpu.CompilerParams(vmem_limit_bytes=LIMIT),
    )(scales, *operands)


NY, NX, NZ, NC = 8, 4, 8, 2
GROUP = [(dx, dc) for dx in range(NX) for dc in range(NC)][1:]


def here():
    return (
        lax.axis_index("region"),
        lax.axis_index("super_0"),
        lax.axis_index("super_1"),
        lax.axis_index("super_2"),
    )


def on_y(d):
    y, x, z, c = here()
    return (lax.rem(y + d, NY), x, z, c)


def on_z(d):
    y, x, z, c = here()
    return (y, x, lax.rem(z + d, NZ), c)


def on_xc(d):
    y, x, z, c = here()
    return (y, lax.rem(x + d[0], NX), z, lax.rem(c + d[1], NC))


def greet(places):
    barrier = pltpu.get_barrier_semaphore()
    for place in places:
        pl.semaphore_signal(barrier, inc=1, device_id=place, device_id_type=MESH)
    pl.semaphore_wait(barrier, len(places))


def send(source, target, sems, n, place):
    copy = pltpu.make_async_remote_copy(
        src_ref=source,
        dst_ref=target,
        send_sem=sems[0].at[n],
        recv_sem=sems[1].at[n],
        device_id=place,
        device_id_type=MESH,
    )
    copy.start()
    return copy


def arrived(copies):
    for copy in copies:
        copy.wait_recv()


def sent(copies):
    for copy in copies:
        copy.wait_send()


def added(own, arrivals_ref):
    return total_of([own] + [arrivals_ref[n] for n in range(arrivals_ref.shape[0])])


def pair_of_sems(count):
    return [pltpu.SemaphoreType.DMA((count,)), pltpu.SemaphoreType.DMA((count,))]


M_ROWS, C_ROWS = 3 * H, 5 * H
M_PART, C_PART = M_ROWS // NY, C_ROWS // NY


def region_kernel(
    mc_ref, gs_ref, prior_hbm,
    corr_ref, share_ref, t2_ref, w_ref,
    m_ref, c_ref, m_in, c_in, g_in, g_sum, y_in, prior_ref, v_ref,
    prior_sem, s0, r0, s1, r1, s2, r2, s3, r3, s4, r4, s5, r5,
    f_ref, *scratch,
):
    y, x, z, c = here()
    prior_copy = pltpu.make_async_copy(prior_hbm, prior_ref, prior_sem)
    prior_copy.start()
    greet([on_y(d) for d in range(1, NY)] + [on_xc(d) for d in GROUP])
    started = []

    def scatter(rows, first, part, target, sems):
        copies = []
        for d in range(1, NY):
            place = on_y(d)
            at = pl.ds(pl.multiple_of(first + place[0] * part, 8), part)
            copies.append(send(rows.at[at, :], target.at[d - 1], sems, d - 1, place))
        started.extend(copies)
        return copies

    def gather(ref, part, sems):
        at = pl.ds(pl.multiple_of(y * part, 8), part)
        copies = [send(ref.at[at, :], ref.at[at, :], sems, d - 1, on_y(d)) for d in range(1, NY)]
        started.extend(copies)
        return copies

    m_scatter = scatter(mc_ref, 0, M_PART, m_in, (s0, r0))
    g_scatter = []
    for n, d in enumerate(GROUP):
        place = on_xc(d)
        g_scatter.append(send(gs_ref.at[place[3], :, place[1]], g_in.at[n], (s1, r1), n, place))
    started.extend(g_scatter)
    arrived(m_scatter)
    own = pl.ds(pl.multiple_of(y * M_PART, 8), M_PART)
    m_ref[own, :] = added(mc_ref[own, :], m_in)
    m_gather = gather(m_ref, M_PART, (s2, r2))
    c_scatter = scatter(mc_ref, M_ROWS, C_PART, c_in, (s3, r3))
    arrived(m_gather)
    prior_copy.wait()
    f_ref[...] = prior_ref[...] + whole_of(m_ref, 0)
    later = {}

    def between():
        arrived(c_scatter)
        mine = pl.ds(pl.multiple_of(y * C_PART, 8), C_PART)
        theirs = pl.ds(pl.multiple_of(M_ROWS + y * C_PART, 8), C_PART)
        c_ref[mine, :] = added(mc_ref[theirs, :], c_in)
        later["c"] = gather(c_ref, C_PART, (s4, r4))
        arrived(g_scatter)
        g_sum[...] = added(gs_ref[c, :, x], g_in)
        later["y"] = []
        for d in range(1, NY):
            place = on_y(d)
            later["y"].append(send(g_sum.at[place[0]], y_in.at[d - 1], (s5, r5), d - 1, place))
        started.extend(later["y"])

    eliminate(f_ref, w_ref, v_ref, *scratch, between=between)
    arrived(later["c"])
    arrived(later["y"])
    share_ref[...] = added(g_sum[y], y_in)
    cross = jnp.concatenate(
        [
            jnp.concatenate([c_ref[(2 * r + n) * H : (2 * r + n + 1) * H, :] for n in range(2)], axis=1)
            for r in range(2)
        ],
        axis=0,
    )
    rhs = jnp.concatenate([cross, fields_of(c_ref, 4)], axis=1)
    t1 = dot(w_ref[...], cross)
    t2 = dot(v_ref[...], rhs)
    t2_ref[...] = t2
    pack_global(corr_ref, dot_t(t1, t2))
    sent(started)


def region(mc, gs, prior):
    sems = []
    for _ in range(6):
        sems += pair_of_sems(7)
    return pl.pallas_call(
        region_kernel,
        name="region",
        out_shape=[shape(4 * H, H), shape(B, H), shape(R, R + FIELDS), shape(R, R)],
        in_specs=[VMEM, VMEM, pl.BlockSpec(memory_space=pl.ANY)],
        out_specs=[VMEM] * 4,
        scratch_shapes=[
            pltpu.VMEM((M_ROWS, H), F32),
            pltpu.VMEM((C_ROWS, H), F32),
            pltpu.VMEM((NY - 1, M_PART, H), F32),
            pltpu.VMEM((NY - 1, C_PART, H), F32),
            pltpu.VMEM((7, NY, B, H), F32),
            pltpu.VMEM((NY, B, H), F32),
            pltpu.VMEM((NY - 1, B, H), F32),
            pltpu.VMEM((R, R), F32),
            pltpu.VMEM((R, R), F32),
            pltpu.SemaphoreType.DMA,
        ] + sems + [pltpu.VMEM((R, R), F32)] + eliminate_scratch()[1:],
        compiler_params=pltpu.CompilerParams(
            vmem_limit_bytes=LIMIT, collective_id=0, has_side_effects=True
        ),
    )(mc, gs, prior)


def upper_kernel(corr_ref, share_ref, out_ref, k_in, z_in, s0, r0, s1, r1, s2, r2, s3, r3, s4, r4):
    y, x, z, c = here()
    greet(
        [on_xc(d) for d in GROUP]
        + [on_z(d) for d in range(1, NZ)]
        + [on_y(d) for d in range(1, NY)]
    )
    started = []
    first = []
    for n, d in enumerate(GROUP):
        place = on_xc(d)
        first.append(send(corr_ref.at[place[3], y, place[1]], k_in.at[n], (s0, r0), n, place))
    arrived(first)
    z_in[z] = share_ref[...] - added(corr_ref[c, y, x], k_in)
    second = [send(z_in.at[z], z_in.at[z], (s1, r1), d - 1, on_z(d)) for d in range(1, NZ)]
    arrived(second)
    out_ref[c, y, x] = total_of([z_in[n] for n in range(NZ)])
    third = [
        send(out_ref.at[c, y, x], out_ref.at[c, y, x], (s2, r2), dx - 1, on_xc((dx, 0)))
        for dx in range(1, NX)
    ]
    arrived(third)
    fourth = [send(out_ref.at[c, y], out_ref.at[c, y], (s3, r3), d - 1, on_y(d)) for d in range(1, NY)]
    fifth = [send(out_ref.at[c, y], out_ref.at[c, y], (s4, r4), 0, on_xc((0, 1)))]
    for d in range(1, NY):
        fourth[d - 1].wait_recv()
        block = out_ref.at[c, lax.rem(y - d + NY, NY)]
        fifth.append(send(block, block, (s4, r4), d, on_xc((0, 1))))
    arrived(fifth)
    sent(first + second + third + fourth + fifth)


def upper_of(corr, share):
    sems = []
    for count in (7, 7, 3, 7, 8):
        sems += pair_of_sems(count)
    return pl.pallas_call(
        upper_kernel,
        name="upper",
        out_shape=shape(NC, NY, NX, B, H),
        in_specs=[VMEM] * 2,
        out_specs=VMEM,
        scratch_shapes=[pltpu.VMEM((7, B, H), F32), pltpu.VMEM((NZ, B, H), F32)] + sems,
        compiler_params=pltpu.CompilerParams(collective_id=1, has_side_effects=True),
    )(corr, share)


def tail_kernel(up_ref, prior_ref, w_r_ref, t2_r_ref, w_l_ref, t2_l_ref, table_ref, out_ref, w_ref, v_ref, f_ref, *scratch):
    f_ref[...] = prior_ref[...] + whole_of(up_ref, 0)
    eliminate(f_ref, w_ref, v_ref, *scratch)
    g = dot_t(w_ref[...], dot(v_ref[...], fields_of(up_ref, 3)))
    r = dot_t(w_r_ref[...], t2_r_ref[:, R:] - dot(t2_r_ref[:, :R], g))
    rest = t2_l_ref[:, 2 * R :] - dot(t2_l_ref[:, : 2 * R], jnp.concatenate([r, g], axis=0))
    l = dot_t(w_l_ref[...], rest)
    out_ref[...] = dot_t(jnp.concatenate([g, r, l], axis=0), table_ref[...])


def tail(up, prior, w_r, t2_r, w_l, t2_l, table):
    return pl.pallas_call(
        tail_kernel,
        name="tail",
        out_shape=shape(FIELDS, table.shape[1]),
        in_specs=[VMEM] * 7,
        out_specs=VMEM,
        scratch_shapes=[pltpu.VMEM((R, R), F32)] * 2 + eliminate_scratch(),
        compiler_params=pltpu.CompilerParams(vmem_limit_bytes=LIMIT),
    )(up, prior, w_r, t2_r, w_l, t2_l, table)


def shards(
    obs_coords,
    obs_values,
    obs_precision,
    site_coords,
    length_scale,
    global_knots,
    region_knots,
    leaf_knots,
    global_prior,
    region_prior,
    leaf_prior,
):
    mc, gs, t2, w, table = leaf(
        length_scale,
        obs_coords,
        obs_values,
        obs_precision[None],
        global_knots,
        region_knots[0],
        leaf_knots[0],
        leaf_prior[0],
        site_coords,
    )
    tiles = (NC, NY, NX, B, H)
    corr, share, t2_r, w_r = region(mc, gs.reshape(tiles), region_prior[0])
    upper = upper_of(corr.reshape(tiles), share)
    return tail(upper.reshape(4 * H, H), global_prior, w_r, t2_r, w, t2, table)


def solution(mesh):
    split = Mesh(
        mesh.devices.reshape(NY, NX, NZ, NC),
        ("region", "super_0", "super_1", "super_2"),
    )
    return jax.shard_map(
        shards,
        mesh=split,
        in_specs=(
            P(None, REGION_SUPER),
            P(None, REGION_SUPER),
            P(REGION_SUPER),
            P(None, REGION_SUPER),
            P(),
            P(),
            P(SUPER, None, None),
            P(REGION_SUPER, None, None),
            P(),
            P(SUPER, None, None),
            P(REGION_SUPER, None, None),
        ),
        out_specs=P(None, REGION_SUPER),
        check_vma=False,
    )
```

time: 422 us -> 124 us (0.29)
  other arithmetic: 174 us -> 0 us
  waiting for transfers between devices: 119 us -> 0 us
  Pallas kernels: 0 us -> 114 us
  blocking collectives: 53.5 us -> 0 us
  matrix products: 21 us -> 0 us
  starting transfers between devices: 17 us -> 0 us
  local copies, waits for them, and re-layouts: 25.7 us -> 10 us
  between operations: 8.84 us -> 0.07 us
    another operation x27 -> x0, other arithmetic: 163 us -> none  [the longest x7 34.7 us: shards(): factor = jnp.linalg.cholesky(global_prior + upper[:, :R])]
    all_to_all x2 -> x0, waiting for transfers between devices: 119 us -> none  [copy_for_each(): return lax.all_to_all(copies, axis, split_axis=0, concat_axis=0, tiled=True)]
    pallas_call x0 -> x4, Pallas kernels: none -> 114 us  [the longest x1 39.8 us: upper_of(): pl.pallas_call(upper_kernel, name='upper', out_shape=shape(NC, NY, NX, B,...]
    all_to_all x3 -> x0, blocking collectives: 53.5 us -> none  [the longest x1 35.6 us: summed_on_arrival(): tiles = lax.all_to_all(in_blocks(x, dim, peers), axis, 0, 0, tiled=True)]
    all_to_all x2 -> x0, starting transfers between devices: 17 us -> none  [copy_for_each(): return lax.all_to_all(copies, axis, split_axis=0, concat_axis=0, tiled=True)]
    dot_general x6 -> x0, matrix products: 14.1 us -> none  [the longest x1 7.95 us: leaf_terms(): lax.dot_general(scaled, scaled, (((0,), (0,)), ((), ())), preferred_eleme...]
    another operation x28 -> x0, local copies, waits for them, and re-layouts: 12.4 us -> none
    unnamed x23 -> x28, local copies, waits for them, and re-layouts: 2.05 us -> 10 us
  transfers between devices with their start and end apart: 2 -> 0, of which waited for: 2 -> 0; matrix products, arithmetic and copies ran while one was open for 0% -> 0% of each run, Pallas kernels for 0% -> 0%
where the time goes in v1:
time: 124 us
  Pallas kernels  114 us (92%)
  local copies, waits for them, and re-layouts  10 us (8%)
    pallas_call x1, Pallas kernels, upper_of(): pl.pallas_call(upper_kernel, name='upper', out_shape=shape(NC, NY, NX, B,...  39.8 us
    pallas_call x1, Pallas kernels, region(): pl.pallas_call(region_kernel, name='region', out_shape=[shape(4 * H, H),...  34.5 us
    pallas_call x1, Pallas kernels, leaf(): pl.pallas_call(leaf_kernel, name='leaf', out_shape=[shape(8 * H, H), shap...  24.1 us
    pallas_call x1, Pallas kernels, tail(): pl.pallas_call(tail_kernel, name='tail', out_shape=shape(FIELDS, table.sh...  15.3 us
    unnamed x28, local copies, waits for them, and re-layouts  10 us

profile of v1, /device:TPU:1, one launch (start us, length us, event | category | flops | bytes accessed | tf_op | source)
XLA Modules:
  0.0 123.7 jit_solution(17473044299545743659)
XLA Ops:
  0.0 0.0 copy-start.1
  0.0 1.0 copy-done.1
  1.0 0.0 copy-start.2
  1.0 0.9 copy-done.2
  2.0 0.0 copy-start.6
  2.0 0.8 copy-done.6
  2.8 0.7 copy-done.7
  3.5 0.7 copy-done.8
  4.2 0.7 copy-done.10
  4.8 0.7 copy-done.11
  5.5 0.7 copy-done.12
  6.2 0.7 copy-done.13
  6.9 24.1 %leaf.1 = (f32[1024,128]{1,0:T(8,128)S(1)}, f32[512,128]{1,0:T(8,128)S(1)}, f32[256,576]{1,0:T(8,128)S(1)}, f32[256,256]{1,0:T(8,128)S(1)}, f32[768,512]{1,0:T(8,128)S(1)}) custom-call(f32[3]{0:T(128)S(1)} %copy-done.13, f32[2,256]{1,0:T(2,128)S(1)} %copy-done.10, f32[2,256]{1,0:T(2,128)S(1)} %bitcast.14, f32[2,256]{1,0:T(2,128)S(1)} %bitcast.15, ...), custom_call_target="tpu_custom_call" | custom-call | tf_op jit(solution)/shard_map/leaf/pallas_call | solution.py:253
  31.0 0.0 copy-start.4
  31.0 0.9 copy-done.4
  31.9 34.5 %region.1 = (f32[512,128]{1,0:T(8,128)S(1)}, f32[8,128]{1,0:T(8,128)S(1)}, f32[256,320]{1,0:T(8,128)S(1)}, f32[256,256]{1,0:T(8,128)S(1)}) custom-call(f32[1024,128]{1,0:T(8,128)S(1)} %get-tuple-element.14.mc_ref, f32[2,8,4,8,128]{4,3,2,1,0:T(8,128)S(1)} %bitcast.12, f32[256,256]{1,0:T(8,128)S(1)} %bitcast.11), custom_call_target="tpu_custom_call" | custom-call | tf_op jit(solution)/shard_map/region/pallas_call | solution.py:426
  66.4 0.0 copy-start.3
  66.4 0.7 copy-done.3
  67.1 0.6 copy-done.9
  67.7 39.8 %upper.1 = f32[2,8,4,8,128]{4,3,2,1,0:T(8,128)} custom-call(f32[2,8,4,8,128]{4,3,2,1,0:T(8,128)} %bitcast.10, f32[8,128]{1,0:T(8,128)} %copy-done.9), custom_call_target="tpu_custom_call" | custom-call | tf_op jit(solution)/shard_map/upper/pallas_call | solution.py:486
  107.5 0.0 copy-done.5
  107.5 0.0 copy-start
  107.5 0.9 copy-done
  108.5 15.3 %tail.1 = f32[64,512]{1,0:T(8,128)} custom-call(f32[512,128]{1,0:T(8,128)S(1)} %bitcast.8, f32[256,256]{1,0:T(8,128)S(1)} %copy-done.5, f32[256,256]{1,0:T(8,128)S(1)} %get-tuple-element.18.w_r_ref, f32[256,320]{1,0:T(8,128)S(1)} %get-tuple-element.19.t2_r_ref, f32[256,256]{1,0:T(8,128)S(1)} %get-tuple-element.20.w_l_ref, ...), custom_call_target="tpu_custom_call" | custom-call | tf_op jit(solution)/shard_map/tail/pallas_call | solution.py:508
  (8 shorter events, 0.0 us)
Async XLA Ops:
  0.0 1.0 copy-start.1
  1.0 0.9 copy-start.2
  2.0 0.8 copy-start.6
  2.8 0.7 copy-start.7
  3.5 0.7 copy-start.8
  4.2 0.7 copy-start.10
  4.8 0.7 copy-start.11
  5.5 0.7 copy-start.12
  6.2 0.7 copy-start.13
  6.9 100.7 %copy-start.5 = (f32[256,256]{1,0:T(8,128)S(1)}, f32[256,256]{1,0:T(8,128)}, u32[]{:S(2)}) copy-start(f32[256,256]{1,0:T(8,128)} %prior_ref.1) | copy-start | bytes 786436
  31.0 1.0 copy-start.4
  66.4 0.7 copy-start.3
  67.1 0.6 copy-start.9
  107.5 1.0 copy-start

commit v2 on v1

v2 whole, which is shorter than its diff:
```python
import functools

import jax
import jax.numpy as jnp
from jax import lax
from jax.experimental import pallas as pl
from jax.experimental.pallas import tpu as pltpu
from jax.sharding import Mesh
from jax.sharding import PartitionSpec as P

R = 256
B = 8
H = 128
FIELDS = 64
F32 = jnp.float32
BF16 = jnp.bfloat16
HIGH = lax.Precision.HIGHEST
MESH = pl.DeviceIdType.MESH
REGION_SUPER = ("region", "super_0", "super_1", "super_2")
SUPER = ("super_0", "super_1", "super_2")
VMEM = pl.BlockSpec(memory_space=pltpu.VMEM)
SMEM = pl.BlockSpec(memory_space=pltpu.SMEM)
LIMIT = 60 * 1024 * 1024


def parts_of(x):
    high = x.astype(BF16).astype(F32)
    rest = x - high
    middle = rest.astype(BF16).astype(F32)
    return high, middle, rest - middle


def left_stack(x):
    h, m, l = parts_of(x)
    return jnp.concatenate([h, h, m, h, l, m], axis=0).astype(BF16)


def right_stack(x):
    h, m, l = parts_of(x)
    return jnp.concatenate([h, m, h, l, h, m], axis=0).astype(BF16)


def total_of(terms):
    terms = list(terms)
    while len(terms) > 1:
        pairs = [terms[i] + terms[i + 1] for i in range(0, len(terms) - 1, 2)]
        terms = pairs + terms[len(pairs) * 2 :]
    return terms[0]


def columns_of(x, first):
    zero = jnp.zeros((B, H), jnp.int32)
    return [jnp.take_along_axis(x, zero + (first + j), axis=1) for j in range(B)]


def row_of(ref, r):
    return jnp.broadcast_to(ref[r : r + 1, :], (B, ref.shape[1]))


def twice(x):
    return jnp.concatenate([x, x], axis=1)


def eliminate(f_ref, w_ref, v_ref, cols_ref, rows_ref, lh_ref, xh_ref, between=None):
    lane = lax.broadcasted_iota(jnp.int32, (B, R), 1)
    sub = lax.broadcasted_iota(jnp.int32, (B, R), 0)
    sub_half = lax.broadcasted_iota(jnp.int32, (B, H), 0)
    lane_all = lax.broadcasted_iota(jnp.int32, (R, R), 1)
    lh_ref[...] = jnp.zeros_like(lh_ref)
    xh_ref[...] = jnp.zeros_like(xh_ref)

    def body(k, panel):
        base = pl.multiple_of(k * B, B)
        half = lax.div(k, 16)
        at = (k - 16 * half) * B
        diag = jnp.where(half == 0, panel[:, :H], panel[:, H:])
        for j, column in enumerate(columns_of(diag, at)):
            cols_ref[j * B : (j + 1) * B, :] = column
        mark = (lane >= base) & (lane < base + B)
        eye = jnp.where(lane == base + sub, 1.0, 0.0).astype(F32)
        rows_ref[...] = jnp.where(mark, eye, panel)
        update = lax.dot_general(
            lh_ref[...], xh_ref[...], (((0,), (0,)), ((), ())), preferred_element_type=F32
        )
        last = (lane_all >= base - B) & (lane_all < base)
        f_ref[...] = jnp.where(last, 0.0, f_ref[...]) - update
        s = {}
        for j in range(B):
            for i in range(j + 1):
                s[i, j] = row_of(cols_ref, j * B + i)
        low = {}
        inv = []
        for p in range(B):
            inv.append(1.0 / s[p, p])
            for i in range(p + 1, B):
                m = s[p, i] * inv[p]
                for j in range(i, B):
                    s[i, j] = s[i, j] - m * s[p, j]
                for c in range(p):
                    low[i, c] = low[i, c] - m * low[p, c]
                low[i, p] = -m
        following = pl.multiple_of(jnp.minimum(k + 1, R // B - 1) * B, B)
        ahead = f_ref[pl.ds(following, B), :]
        g = columns_of(jnp.where(half == 0, ahead[:, :H], ahead[:, H:]), at)
        rows = [row_of(rows_ref, j) for j in range(B)]
        row = [total_of([twice(low[j, m]) * rows[m] for m in range(j)] + [rows[j]]) for j in range(B)]
        lcol = [total_of([g[m] * low[j, m] for m in range(j)] + [g[j]]) * inv[j] for j in range(B)]
        panel_next = jnp.where(mark, 0.0, ahead) - total_of(
            [twice(lcol[j]) * row[j] for j in range(B)]
        )
        dcol = inv[0]
        mine = row[0]
        for i in range(1, B):
            dcol = jnp.where(sub_half == i, inv[i], dcol)
            mine = jnp.where(sub == i, row[i], mine)
        x = twice(dcol) * mine
        done = lane < base + B
        w_ref[pl.ds(base, B), :] = jnp.where(done, mine, 0.0)
        v_ref[pl.ds(base, B), :] = jnp.where(done, x, 0.0)
        lh_ref[...] = left_stack(jnp.where(done, 0.0, mine))
        xh_ref[...] = right_stack(x)
        return panel_next

    if between is None:
        lax.fori_loop(0, R // B, body, f_ref[0:B, :])
    else:
        panel = lax.fori_loop(0, R // B // 2, body, f_ref[0:B, :])
        between()
        lax.fori_loop(R // B // 2, R // B, body, panel)


def eliminate_scratch():
    return [
        pltpu.VMEM((R, R), F32),
        pltpu.VMEM((B * B, H), F32),
        pltpu.VMEM((B, R), F32),
        pltpu.VMEM((48, R), BF16),
        pltpu.VMEM((48, R), BF16),
    ]


def dot(a, b):
    return jnp.dot(a, b, precision=HIGH, preferred_element_type=F32)


def dot_t(a, b):
    return lax.dot_general(a, b, (((0,), (0,)), ((), ())), precision=HIGH, preferred_element_type=F32)


def gram_of(a, b):
    return lax.dot_general(a, b, (((1,), (1,)), ((), ())), preferred_element_type=F32)


def upright(knots):
    spare = jnp.zeros((6, R), F32)
    return jnp.concatenate([knots, spare], axis=0).T


def basis(knots, places, scale):
    diff_x = knots[:, 0:1] - places[0:1, :]
    diff_y = knots[:, 1:2] - places[1:2, :]
    return jnp.exp((diff_x * diff_x + diff_y * diff_y) * scale)


def factors(scale_ref):
    return [-0.5 / (scale_ref[i] * scale_ref[i]) for i in range(3)]


CHUNK = 512


def pack_global(out_ref, upper):
    rows = [
        upper[:H, :H],
        upper[H:, :H],
        upper[H:, H:R],
        jnp.concatenate([upper[:H, R:], upper[H:, R:]], axis=1),
    ]
    out_ref[...] = jnp.concatenate(rows, axis=0).reshape(out_ref.shape)


def whole_of(ref, first):
    a, b, c = (ref[(first + n) * H : (first + n + 1) * H, :] for n in range(3))
    return jnp.concatenate(
        [jnp.concatenate([a, b.T], axis=1), jnp.concatenate([b, c], axis=1)], axis=0
    )


def fields_of(ref, block):
    y = ref[block * H : (block + 1) * H, :]
    return jnp.concatenate([y[:, :FIELDS], y[:, FIELDS:]], axis=0)


def shape(*dims):
    return jax.ShapeDtypeStruct(dims, F32)


NY, NX, NZ, NC = 8, 4, 8, 2
GROUP = [(dx, dc) for dx in range(NX) for dc in range(NC)][1:]


def here():
    return (
        lax.axis_index("region"),
        lax.axis_index("super_0"),
        lax.axis_index("super_1"),
        lax.axis_index("super_2"),
    )


def on_y(d):
    y, x, z, c = here()
    return (lax.rem(y + d, NY), x, z, c)


def on_z(d):
    y, x, z, c = here()
    return (y, x, lax.rem(z + d, NZ), c)


def on_xc(d):
    y, x, z, c = here()
    return (y, lax.rem(x + d[0], NX), z, lax.rem(c + d[1], NC))


def greet(places):
    barrier = pltpu.get_barrier_semaphore()
    for place in places:
        pl.semaphore_signal(barrier, inc=1, device_id=place, device_id_type=MESH)
    return lambda: pl.semaphore_wait(barrier, len(places))


def send(source, target, sems, n, place):
    copy = pltpu.make_async_remote_copy(
        src_ref=source,
        dst_ref=target,
        send_sem=sems[0].at[n],
        recv_sem=sems[1].at[n],
        device_id=place,
        device_id_type=MESH,
    )
    copy.start()
    return copy


def arrived(copies):
    for copy in copies:
        copy.wait_recv()


def sent(copies):
    for copy in copies:
        copy.wait_send()


def added(own, arrivals_ref):
    return total_of([own] + [arrivals_ref[n] for n in range(arrivals_ref.shape[0])])


def pair_of_sems(count):
    return [pltpu.SemaphoreType.DMA((count,)), pltpu.SemaphoreType.DMA((count,))]


M_ROWS, C_ROWS = 3 * H, 5 * H
M_PART, C_PART = M_ROWS // NY, C_ROWS // NY
EXCHANGES = (7, 7, 7, 7, 7, 7, 7, 7, 3, 7, 8)


def kernel(*refs):
    it = iter(refs)
    take = lambda n: [next(it) for _ in range(n)]
    (scale_ref,) = take(1)
    sources = take(10)
    (out_ref,) = take(1)
    targets = take(10)
    (copy_sems,) = take(1)
    sems = [take(2) for _ in EXCHANGES]
    z_ref, gv_ref, gr_ref, gg_ref, w_ref, v_ref, t2_ref, table_ref = take(8)
    mc_ref, gs_ref, m_ref, c_ref, m_in, c_in, g_in, g_sum, y_in = take(9)
    corr_ref, k_in, z_in, up_ref = take(4)
    elim = take(5)
    f_ref = elim[0]
    gk_ref, rk_ref, lk_ref, coords_ref, precision_ref, values_ref, sites_ref, prior_l, prior_r, prior_g = targets

    copies = [
        pltpu.make_async_copy(a, b, copy_sems.at[n]) for n, (a, b) in enumerate(zip(sources, targets))
    ]
    for copy in copies:
        copy.start()
    y, x, z, c = here()
    met = greet(
        [on_y(d) for d in range(1, NY)]
        + [on_xc(d) for d in GROUP]
        + [on_z(d) for d in range(1, NZ)]
    )
    for copy in copies[:6]:
        copy.wait()
    started = []

    scale = factors(scale_ref)
    knots = [upright(lk_ref[...]), upright(rk_ref[...]), upright(gk_ref[...])]
    scales = [scale[2], scale[1], scale[0]]
    gv_ref[...] = jnp.zeros_like(gv_ref)
    gr_ref[...] = jnp.zeros_like(gr_ref)
    gg_ref[...] = jnp.zeros_like(gg_ref)

    def step(i, _):
        at = pl.ds(pl.multiple_of(i * CHUNK, CHUNK), CHUNK)
        places = coords_ref[:, at]
        weight = jnp.sqrt(precision_ref[:, at])
        for n in range(3):
            z_ref[n * R : (n + 1) * R, :] = (basis(knots[n], places, scales[n]) * weight).astype(BF16)
        z_ref[3 * R :, :] = (values_ref[:, at].astype(F32) * weight).astype(BF16)
        gv_ref[...] += gram_of(z_ref[:R, :], z_ref[...])
        gr_ref[...] += gram_of(z_ref[R : 2 * R, :], z_ref[R:, :])
        gg_ref[...] += gram_of(z_ref[2 * R : 3 * R, :], z_ref[2 * R :, :])
        return 0

    lax.fori_loop(0, coords_ref.shape[1] // CHUNK, step, 0)
    for copy in copies[6:]:
        copy.wait()
    f_ref[...] = prior_l[...] + gv_ref[:, :R]
    eliminate(*elim[:1], w_ref, v_ref, *elim[1:])

    def scatter(rows, first, part, target, pair):
        copies = []
        for d in range(1, NY):
            place = on_y(d)
            at = pl.ds(pl.multiple_of(first + place[0] * part, 8), part)
            copies.append(send(rows.at[at, :], target.at[d - 1], pair, d - 1, place))
        started.extend(copies)
        return copies

    def gather(ref, part, pair):
        at = pl.ds(pl.multiple_of(y * part, 8), part)
        copies = [send(ref.at[at, :], ref.at[at, :], pair, d - 1, on_y(d)) for d in range(1, NY)]
        started.extend(copies)
        return copies

    t1 = dot(w_ref[...], gv_ref[:, R : 2 * R])
    t2_ref[:, :R] = dot(v_ref[...], gv_ref[:, R : 2 * R])
    regional = gr_ref[:, :R] - dot_t(t1, t2_ref[:, :R])
    mc_ref[0:H, :] = regional[:H, :H]
    mc_ref[H : 2 * H, :] = regional[H:, :H]
    mc_ref[2 * H : 3 * H, :] = regional[H:, H:R]
    met()
    m_scatter = scatter(mc_ref, 0, M_PART, m_in, sems[0])
    t2_ref[:, R:] = dot(v_ref[...], gv_ref[:, 2 * R :])
    regional = gr_ref[:, R:] - dot_t(t1, t2_ref[:, R:])
    for r in range(2):
        for n in range(2):
            k = 3 + 2 * r + n
            mc_ref[k * H : (k + 1) * H, :] = regional[r * H : (r + 1) * H, n * H : (n + 1) * H]
    mc_ref[7 * H :, :] = jnp.concatenate([regional[:H, R:], regional[H:, R:]], axis=1)
    t1 = dot(w_ref[...], gv_ref[:, 2 * R : 3 * R])
    pack_global(gs_ref, gg_ref[...] - dot_t(t1, t2_ref[:, R:]))
    g_scatter = []
    for n, d in enumerate(GROUP):
        place = on_xc(d)
        g_scatter.append(send(gs_ref.at[place[3], :, place[1]], g_in.at[n], sems[1], n, place))
    started.extend(g_scatter)
    arrived(m_scatter)
    own = pl.ds(pl.multiple_of(y * M_PART, 8), M_PART)
    m_ref[own, :] = added(mc_ref[own, :], m_in)
    m_gather = gather(m_ref, M_PART, sems[2])
    c_scatter = scatter(mc_ref, M_ROWS, C_PART, c_in, sems[3])

    places = sites_ref[...]
    sites_l = dot(w_ref[...], basis(knots[0], places, scales[0]))
    seen = dot_t(t2_ref[...], sites_l)
    table_ref[:R, :] = basis(knots[1], places, scales[1]) - seen[:R]
    table_ref[R : 2 * R, :] = basis(knots[2], places, scales[2]) - seen[R : 2 * R]
    table_ref[2 * R :, :] = seen[2 * R :]

    arrived(m_gather)
    f_ref[...] = prior_r[...] + whole_of(m_ref, 0)
    later = {}

    def between():
        arrived(c_scatter)
        mine = pl.ds(pl.multiple_of(y * C_PART, 8), C_PART)
        theirs = pl.ds(pl.multiple_of(M_ROWS + y * C_PART, 8), C_PART)
        c_ref[mine, :] = added(mc_ref[theirs, :], c_in)
        later["c"] = gather(c_ref, C_PART, sems[4])
        arrived(g_scatter)
        g_sum[...] = added(gs_ref[c, :, x], g_in)
        later["y"] = []
        for d in range(1, NY):
            place = on_y(d)
            later["y"].append(send(g_sum.at[place[0]], y_in.at[d - 1], sems[5], d - 1, place))
        started.extend(later["y"])

    eliminate(*elim[:1], w_ref, v_ref, *elim[1:], between=between)
    arrived(later["c"])
    cross = jnp.concatenate(
        [
            jnp.concatenate([c_ref[(2 * r + n) * H : (2 * r + n + 1) * H, :] for n in range(2)], axis=1)
            for r in range(2)
        ],
        axis=0,
    )
    t1 = dot(w_ref[...], cross)
    t2_ref[:, : R + FIELDS] = dot(v_ref[...], jnp.concatenate([cross, fields_of(c_ref, 4)], axis=1))
    pack_global(corr_ref, dot_t(t1, t2_ref[:, : R + FIELDS]))

    first = []
    for n, d in enumerate(GROUP):
        place = on_xc(d)
        first.append(send(corr_ref.at[place[3], y, place[1]], k_in.at[n], sems[6], n, place))
    arrived(later["y"])
    share = added(g_sum[y], y_in)
    arrived(first)
    z_in[z] = share - added(corr_ref[c, y, x], k_in)
    second = [send(z_in.at[z], z_in.at[z], sems[7], d - 1, on_z(d)) for d in range(1, NZ)]
    sites_r = dot(w_ref[...], table_ref[:R, :])
    seen = dot_t(t2_ref[:, : R + FIELDS], sites_r)
    table_ref[R : 2 * R, :] -= seen[:R]
    table_ref[2 * R :, :] += seen[R:]
    arrived(second)
    up_ref[c, y, x] = total_of([z_in[n] for n in range(NZ)])
    third = [
        send(up_ref.at[c, y, x], up_ref.at[c, y, x], sems[8], dx - 1, on_xc((dx, 0)))
        for dx in range(1, NX)
    ]
    arrived(third)
    fourth = [send(up_ref.at[c, y], up_ref.at[c, y], sems[9], d - 1, on_y(d)) for d in range(1, NY)]
    fifth = [send(up_ref.at[c, y], up_ref.at[c, y], sems[10], 0, on_xc((0, 1)))]
    for d in range(1, NY):
        fourth[d - 1].wait_recv()
        block = up_ref.at[c, lax.rem(y - d + NY, NY)]
        fifth.append(send(block, block, sems[10], d, on_xc((0, 1))))
    arrived(fifth)
    upper = up_ref[...].reshape(4 * H, H)
    f_ref[...] = prior_g[...] + whole_of(upper, 0)
    eliminate(*elim[:1], w_ref, v_ref, *elim[1:])
    g = dot_t(w_ref[...], dot(v_ref[...], fields_of(upper, 3)))
    out_ref[...] = table_ref[2 * R :, :] + dot_t(g, table_ref[R : 2 * R, :])
    sent(started + first + second + third + fourth + fifth)


def everything(scales, *operands):
    sites = operands[6]
    sems = []
    for count in EXCHANGES:
        sems += pair_of_sems(count)
    tiles = pltpu.VMEM((NC, NY, NX, B, H), F32)
    return pl.pallas_call(
        kernel,
        name="all",
        out_shape=shape(FIELDS, sites.shape[1]),
        in_specs=[SMEM] + [pl.BlockSpec(memory_space=pl.ANY)] * len(operands),
        out_specs=VMEM,
        scratch_shapes=[pltpu.VMEM(a.shape, a.dtype) for a in operands]
        + [pltpu.SemaphoreType.DMA((len(operands),))]
        + sems
        + [
            pltpu.VMEM((3 * R + FIELDS, CHUNK), BF16),
            pltpu.VMEM((R, 3 * R + FIELDS), F32),
            pltpu.VMEM((R, 2 * R + FIELDS), F32),
            pltpu.VMEM((R, R + FIELDS), F32),
            pltpu.VMEM((R, R), F32),
            pltpu.VMEM((R, R), F32),
            pltpu.VMEM((R, 2 * R + FIELDS), F32),
            pltpu.VMEM((2 * R + FIELDS, sites.shape[1]), F32),
            pltpu.VMEM((8 * H, H), F32),
            tiles,
            pltpu.VMEM((M_ROWS, H), F32),
            pltpu.VMEM((C_ROWS, H), F32),
            pltpu.VMEM((NY - 1, M_PART, H), F32),
            pltpu.VMEM((NY - 1, C_PART, H), F32),
            pltpu.VMEM((7, NY, B, H), F32),
            pltpu.VMEM((NY, B, H), F32),
            pltpu.VMEM((NY - 1, B, H), F32),
            tiles,
            pltpu.VMEM((7, B, H), F32),
            pltpu.VMEM((NZ, B, H), F32),
            tiles,
        ]
        + eliminate_scratch(),
        compiler_params=pltpu.CompilerParams(
            vmem_limit_bytes=LIMIT, collective_id=0, has_side_effects=True
        ),
    )(scales, *operands)


def shards(
    obs_coords,
    obs_values,
    obs_precision,
    site_coords,
    length_scale,
    global_knots,
    region_knots,
    leaf_knots,
    global_prior,
    region_prior,
    leaf_prior,
):
    return everything(
        length_scale,
        global_knots,
        region_knots[0],
        leaf_knots[0],
        obs_coords,
        obs_precision[None],
        obs_values,
        site_coords,
        leaf_prior[0],
        region_prior[0],
        global_prior,
    )


def solution(mesh):
    split = Mesh(
        mesh.devices.reshape(NY, NX, NZ, NC),
        ("region", "super_0", "super_1", "super_2"),
    )
    return jax.shard_map(
        shards,
        mesh=split,
        in_specs=(
            P(None, REGION_SUPER),
            P(None, REGION_SUPER),
            P(REGION_SUPER),
            P(None, REGION_SUPER),
            P(),
            P(),
            P(SUPER, None, None),
            P(REGION_SUPER, None, None),
            P(),
            P(SUPER, None, None),
            P(REGION_SUPER, None, None),
        ),
        out_specs=P(None, REGION_SUPER),
        check_vma=False,
    )
```

time: 124 us -> 101 us (0.81)
  Pallas kernels: 114 us -> 98.9 us
  local copies, waits for them, and re-layouts: 10 us -> 1.57 us
    pallas_call x4 -> x1, Pallas kernels: 114 us -> 98.9 us  [everything(): pl.pallas_call(kernel, name='all', out_shape=shape(FIELDS, sites.shape[1]...]
    unnamed x28 -> x1, local copies, waits for them, and re-layouts: 10 us -> 1.57 us
where the time goes in v2:
time: 101 us; the launch traced here: 100 us
  Pallas kernels  98.9 us (98%)
  local copies, waits for them, and re-layouts  1.57 us (2%)
    pallas_call x1, Pallas kernels, everything(): pl.pallas_call(kernel, name='all', out_shape=shape(FIELDS, sites.shape[1]...  98.9 us

profile of v2, /device:TPU:1, one launch (start us, length us, event | category | flops | bytes accessed | tf_op | source)
XLA Modules:
  0.0 100.4 jit_solution(12265548239153232486)
XLA Ops:
  0.0 98.9 %all.1 = f32[64,512]{1,0:T(8,128)} custom-call(f32[3]{0:T(128)} %refs_0_.1, f32[2,256]{1,0:T(2,128)} %refs_1_.1, f32[2,256]{1,0:T(2,128)} %bitcast.8, f32[2,256]{1,0:T(2,128)} %bitcast.9, f32[2,4096]{1,0:T(2,128)} %refs_4_.1, f32[1,4096]{1,0:T(1,128)} %bitcast.7, bf16[64,4096]{1,0:T(8,128)(2,1)} %refs_6_.1, f32[2,512]{1,0:T(2,128)} %refs_7_.1, ...), custom_call_target="tpu_custom_call" | custom-call | tf_op jit(solution)/shard_map/all/pallas_call | solution.py:447
  98.9 1.6 %copy.13 = f32[64,512]{1,0:T(8,128)} copy(f32[64,512]{1,0:T(8,128)} %all.1) | data formatting | bytes 262144

commit v3 on v2

--- a/solution.py
+++ b/solution.py
@@ -61,15 +61,14 @@
     return jnp.concatenate([x, x], axis=1)
 
 
-def eliminate(f_ref, w_ref, v_ref, cols_ref, rows_ref, lh_ref, xh_ref, between=None):
+def eliminate(f_ref, w_ref, v_ref, cols_ref, rows_ref, mine_ref, x_ref, lh_ref, xh_ref, hooks=()):
     lane = lax.broadcasted_iota(jnp.int32, (B, R), 1)
     sub = lax.broadcasted_iota(jnp.int32, (B, R), 0)
     sub_half = lax.broadcasted_iota(jnp.int32, (B, H), 0)
-    lane_all = lax.broadcasted_iota(jnp.int32, (R, R), 1)
-    lh_ref[...] = jnp.zeros_like(lh_ref)
-    xh_ref[...] = jnp.zeros_like(xh_ref)
-
-    def body(k, panel):
+    for ref in (mine_ref, x_ref, lh_ref, xh_ref):
+        ref[...] = jnp.zeros_like(ref)
+
+    def body(first, k, panel):
         base = pl.multiple_of(k * B, B)
         half = lax.div(k, 16)
         at = (k - 16 * half) * B
@@ -79,11 +78,23 @@
         mark = (lane >= base) & (lane < base + B)
         eye = jnp.where(lane == base + sub, 1.0, 0.0).astype(F32)
         rows_ref[...] = jnp.where(mark, eye, panel)
-        update = lax.dot_general(
-            lh_ref[...], xh_ref[...], (((0,), (0,)), ((), ())), preferred_element_type=F32
+        following = pl.multiple_of(jnp.minimum(k + 1, R // B - 1) * B, B)
+        ahead = f_ref[pl.ds(following, B), :]
+        next_half = lax.div(following, H)
+        next_at = following - next_half * H + sub_half
+
+        def upright_of(row):
+            part = jnp.where(next_half == 0, row[:, :H], row[:, H:])
+            return jnp.take_along_axis(part, next_at, axis=1)
+
+        keep = jnp.where((lane >= base - B) & (lane < base), 0.0, 1.0).astype(F32)
+        before = [upright_of(row_of(mine_ref, j)) for j in range(B)]
+        ahead = ahead * keep - total_of([twice(before[j]) * row_of(x_ref, j) for j in range(B)])
+        f_ref[first:, :] = f_ref[first:, :] * keep[0:1, :] - lax.dot_general(
+            lh_ref[:, first:], xh_ref[...], (((0,), (0,)), ((), ())), preferred_element_type=F32
         )
-        last = (lane_all >= base - B) & (lane_all < base)
-        f_ref[...] = jnp.where(last, 0.0, f_ref[...]) - update
+        rows = [row_of(rows_ref, j) for j in range(B)]
+        g = [upright_of(row) for row in rows]
         s = {}
         for j in range(B):
             for i in range(j + 1):
@@ -99,15 +110,9 @@
                 for c in range(p):
                     low[i, c] = low[i, c] - m * low[p, c]
                 low[i, p] = -m
-        following = pl.multiple_of(jnp.minimum(k + 1, R // B - 1) * B, B)
-        ahead = f_ref[pl.ds(following, B), :]
-        g = columns_of(jnp.where(half == 0, ahead[:, :H], ahead[:, H:]), at)
-        rows = [row_of(rows_ref, j) for j in range(B)]
         row = [total_of([twice(low[j, m]) * rows[m] for m in range(j)] + [rows[j]]) for j in range(B)]
         lcol = [total_of([g[m] * low[j, m] for m in range(j)] + [g[j]]) * inv[j] for j in range(B)]
-        panel_next = jnp.where(mark, 0.0, ahead) - total_of(
-            [twice(lcol[j]) * row[j] for j in range(B)]
-        )
+        panel_next = jnp.where(mark, 0.0, ahead) - total_of([twice(lcol[j]) * row[j] for j in range(B)])
         dcol = inv[0]
         mine = row[0]
         for i in range(1, B):
@@ -117,16 +122,21 @@
         done = lane < base + B
         w_ref[pl.ds(base, B), :] = jnp.where(done, mine, 0.0)
         v_ref[pl.ds(base, B), :] = jnp.where(done, x, 0.0)
+        mine_ref[...] = mine
+        x_ref[...] = x
         lh_ref[...] = left_stack(jnp.where(done, 0.0, mine))
         xh_ref[...] = right_stack(x)
         return panel_next
 
-    if between is None:
-        lax.fori_loop(0, R // B, body, f_ref[0:B, :])
-    else:
-        panel = lax.fori_loop(0, R // B // 2, body, f_ref[0:B, :])
-        between()
-        lax.fori_loop(R // B // 2, R // B, body, panel)
+    panel = f_ref[0:B, :]
+    at = 0
+    for stop, hook in sorted([*hooks, (R // B // 2, None), (R // B, None)], key=lambda h: h[0]):
+        if stop > at:
+            first = H if at >= R // B // 2 else 0
+            panel = lax.fori_loop(at, stop, functools.partial(body, first), panel)
+            at = stop
+        if hook is not None:
+            hook()
 
 
 def eliminate_scratch():
@@ -134,6 +144,8 @@
         pltpu.VMEM((R, R), F32),
         pltpu.VMEM((B * B, H), F32),
         pltpu.VMEM((B, R), F32),
+        pltpu.VMEM((B, R), F32),
+        pltpu.VMEM((B, R), F32),
         pltpu.VMEM((48, R), BF16),
         pltpu.VMEM((48, R), BF16),
     ]
@@ -166,7 +178,7 @@
     return [-0.5 / (scale_ref[i] * scale_ref[i]) for i in range(3)]
 
 
-CHUNK = 512
+CHUNK = 1024
 
 
 def pack_global(out_ref, upper):
@@ -197,6 +209,8 @@
 
 NY, NX, NZ, NC = 8, 4, 8, 2
 GROUP = [(dx, dc) for dx in range(NX) for dc in range(NC)][1:]
+NEAREST = sorted(range(NY), key=lambda d: min(d, NY - d))
+PLANE = [(dx, dy) for dy in NEAREST[::-1] for dx in range(NX) if (dx, dy) != (0, 0)]
 
 
 def here():
@@ -221,6 +235,11 @@
 def on_xc(d):
     y, x, z, c = here()
     return (y, lax.rem(x + d[0], NX), z, lax.rem(c + d[1], NC))
+
+
+def on_xy(d):
+    y, x, z, c = here()
+    return (lax.rem(y + d[1], NY), lax.rem(x + d[0], NX), z, c)
 
 
 def greet(places):
@@ -263,7 +282,8 @@
 
 M_ROWS, C_ROWS = 3 * H, 5 * H
 M_PART, C_PART = M_ROWS // NY, C_ROWS // NY
-EXCHANGES = (7, 7, 7, 7, 7, 7, 7, 7, 3, 7, 8)
+EXCHANGES = (7, 7, 7, 7, 7, 7, 7, 7, 31, 8)
+CROSS_STEP = 0
 
 
 def kernel(*refs):
@@ -275,10 +295,11 @@
     targets = take(10)
     (copy_sems,) = take(1)
     sems = [take(2) for _ in EXCHANGES]
-    z_ref, gv_ref, gr_ref, gg_ref, w_ref, v_ref, t2_ref, table_ref = take(8)
+    z_refs = take(2)
+    gv_ref, gr_ref, gg_ref, w_ref, v_ref, t2_ref, table_ref = take(7)
     mc_ref, gs_ref, m_ref, c_ref, m_in, c_in, g_in, g_sum, y_in = take(9)
     corr_ref, k_in, z_in, up_ref = take(4)
-    elim = take(5)
+    elim = take(7)
     f_ref = elim[0]
     gk_ref, rk_ref, lk_ref, coords_ref, precision_ref, values_ref, sites_ref, prior_l, prior_r, prior_g = targets
 
@@ -289,8 +310,8 @@
         copy.start()
     y, x, z, c = here()
     met = greet(
-        [on_y(d) for d in range(1, NY)]
-        + [on_xc(d) for d in GROUP]
+        [on_xy(d) for d in PLANE]
+        + [on_xc(d) for d in GROUP if d[1]]
         + [on_z(d) for d in range(1, NZ)]
     )
     for copy in copies[:6]:
@@ -300,26 +321,30 @@
     scale = factors(scale_ref)
     knots = [upright(lk_ref[...]), upright(rk_ref[...]), upright(gk_ref[...])]
     scales = [scale[2], scale[1], scale[0]]
-    gv_ref[...] = jnp.zeros_like(gv_ref)
-    gr_ref[...] = jnp.zeros_like(gr_ref)
-    gg_ref[...] = jnp.zeros_like(gg_ref)
-
-    def step(i, _):
-        at = pl.ds(pl.multiple_of(i * CHUNK, CHUNK), CHUNK)
+    grams = (gv_ref, gr_ref, gg_ref)
+    chunks = coords_ref.shape[1] // CHUNK
+
+    def fill(z_ref, i):
+        at = pl.ds(i * CHUNK, CHUNK)
         places = coords_ref[:, at]
         weight = jnp.sqrt(precision_ref[:, at])
+        z_ref[:FIELDS, :] = (values_ref[:, at].astype(F32) * weight).astype(BF16)
         for n in range(3):
-            z_ref[n * R : (n + 1) * R, :] = (basis(knots[n], places, scales[n]) * weight).astype(BF16)
-        z_ref[3 * R :, :] = (values_ref[:, at].astype(F32) * weight).astype(BF16)
-        gv_ref[...] += gram_of(z_ref[:R, :], z_ref[...])
-        gr_ref[...] += gram_of(z_ref[R : 2 * R, :], z_ref[R:, :])
-        gg_ref[...] += gram_of(z_ref[2 * R : 3 * R, :], z_ref[2 * R :, :])
-        return 0
-
-    lax.fori_loop(0, coords_ref.shape[1] // CHUNK, step, 0)
+            first = FIELDS + n * R
+            z_ref[first : first + R, :] = (basis(knots[n], places, scales[n]) * weight).astype(BF16)
+
+    fill(z_refs[0], 0)
+    for i in range(chunks):
+        now, later = z_refs[i % 2], z_refs[(i + 1) % 2]
+        if i + 1 < chunks:
+            fill(later, i + 1)
+        for n, ref in enumerate(grams):
+            first = FIELDS + n * R
+            block = gram_of(now[: first + R, :], now[first : first + R, :])
+            ref[...] = block if i == 0 else ref[...] + block
     for copy in copies[6:]:
         copy.wait()
-    f_ref[...] = prior_l[...] + gv_ref[:, :R]
+    f_ref[...] = prior_l[...] + gv_ref[FIELDS:, :]
     eliminate(*elim[:1], w_ref, v_ref, *elim[1:])
 
     def scatter(rows, first, part, target, pair):
@@ -337,23 +362,30 @@
         started.extend(copies)
         return copies
 
-    t1 = dot(w_ref[...], gv_ref[:, R : 2 * R])
-    t2_ref[:, :R] = dot(v_ref[...], gv_ref[:, R : 2 * R])
-    regional = gr_ref[:, :R] - dot_t(t1, t2_ref[:, :R])
+    leaf_rows = slice(FIELDS, FIELDS + R)
+    region_rows = slice(FIELDS + R, FIELDS + 2 * R)
+    t1 = dot(w_ref[...], gr_ref[leaf_rows, :])
+    t2_ref[:, :R] = dot(v_ref[...], gr_ref[leaf_rows, :])
+    regional = gr_ref[region_rows, :] - dot_t(t1, t2_ref[:, :R])
     mc_ref[0:H, :] = regional[:H, :H]
     mc_ref[H : 2 * H, :] = regional[H:, :H]
     mc_ref[2 * H : 3 * H, :] = regional[H:, H:R]
     met()
     m_scatter = scatter(mc_ref, 0, M_PART, m_in, sems[0])
-    t2_ref[:, R:] = dot(v_ref[...], gv_ref[:, 2 * R :])
-    regional = gr_ref[:, R:] - dot_t(t1, t2_ref[:, R:])
+    right = jnp.concatenate([gg_ref[leaf_rows, :], gv_ref[:FIELDS, :].T], axis=1)
+    t2_ref[:, R:] = dot(v_ref[...], right)
+    regional = jnp.concatenate([gg_ref[region_rows, :], gr_ref[:FIELDS, :].T], axis=1) - dot_t(
+        t1, t2_ref[:, R:]
+    )
     for r in range(2):
         for n in range(2):
             k = 3 + 2 * r + n
             mc_ref[k * H : (k + 1) * H, :] = regional[r * H : (r + 1) * H, n * H : (n + 1) * H]
     mc_ref[7 * H :, :] = jnp.concatenate([regional[:H, R:], regional[H:, R:]], axis=1)
-    t1 = dot(w_ref[...], gv_ref[:, 2 * R : 3 * R])
-    pack_global(gs_ref, gg_ref[...] - dot_t(t1, t2_ref[:, R:]))
+    c_scatter = scatter(mc_ref, M_ROWS, C_PART, c_in, sems[3])
+    t1 = dot(w_ref[...], gg_ref[leaf_rows, :])
+    upper = jnp.concatenate([gg_ref[FIELDS + 2 * R :, :], gg_ref[:FIELDS, :].T], axis=1)
+    pack_global(gs_ref, upper - dot_t(t1, t2_ref[:, R:]))
     g_scatter = []
     for n, d in enumerate(GROUP):
         place = on_xc(d)
@@ -363,7 +395,6 @@
     own = pl.ds(pl.multiple_of(y * M_PART, 8), M_PART)
     m_ref[own, :] = added(mc_ref[own, :], m_in)
     m_gather = gather(m_ref, M_PART, sems[2])
-    c_scatter = scatter(mc_ref, M_ROWS, C_PART, c_in, sems[3])
 
     places = sites_ref[...]
     sites_l = dot(w_ref[...], basis(knots[0], places, scales[0]))
@@ -376,12 +407,14 @@
     f_ref[...] = prior_r[...] + whole_of(m_ref, 0)
     later = {}
 
-    def between():
+    def send_cross():
         arrived(c_scatter)
         mine = pl.ds(pl.multiple_of(y * C_PART, 8), C_PART)
         theirs = pl.ds(pl.multiple_of(M_ROWS + y * C_PART, 8), C_PART)
         c_ref[mine, :] = added(mc_ref[theirs, :], c_in)
         later["c"] = gather(c_ref, C_PART, sems[4])
+
+    def send_share():
         arrived(g_scatter)
         g_sum[...] = added(gs_ref[c, :, x], g_in)
         later["y"] = []
@@ -390,7 +423,7 @@
             later["y"].append(send(g_sum.at[place[0]], y_in.at[d - 1], sems[5], d - 1, place))
         started.extend(later["y"])
 
-    eliminate(*elim[:1], w_ref, v_ref, *elim[1:], between=between)
+    eliminate(*elim[:1], w_ref, v_ref, *elim[1:], hooks=[(CROSS_STEP, send_cross), (20, send_share)])
     arrived(later["c"])
     cross = jnp.concatenate(
         [
@@ -418,24 +451,23 @@
     table_ref[2 * R :, :] += seen[R:]
     arrived(second)
     up_ref[c, y, x] = total_of([z_in[n] for n in range(NZ)])
-    third = [
-        send(up_ref.at[c, y, x], up_ref.at[c, y, x], sems[8], dx - 1, on_xc((dx, 0)))
-        for dx in range(1, NX)
-    ]
-    arrived(third)
-    fourth = [send(up_ref.at[c, y], up_ref.at[c, y], sems[9], d - 1, on_y(d)) for d in range(1, NY)]
-    fifth = [send(up_ref.at[c, y], up_ref.at[c, y], sems[10], 0, on_xc((0, 1)))]
-    for d in range(1, NY):
-        fourth[d - 1].wait_recv()
-        block = up_ref.at[c, lax.rem(y - d + NY, NY)]
-        fifth.append(send(block, block, sems[10], d, on_xc((0, 1))))
-    arrived(fifth)
+    third = {}
+    for n, d in enumerate(PLANE):
+        third[d] = send(up_ref.at[c, y, x], up_ref.at[c, y, x], sems[8], n, on_xy(d))
+    fourth = []
+    for dy in NEAREST:
+        for dx in range(NX):
+            if (dx, dy) != (0, 0):
+                third[dx, dy].wait_recv()
+        block = up_ref.at[c, lax.rem(y - dy + NY, NY)]
+        fourth.append(send(block, block, sems[9], dy, on_xc((0, 1))))
+    arrived(fourth)
     upper = up_ref[...].reshape(4 * H, H)
     f_ref[...] = prior_g[...] + whole_of(upper, 0)
     eliminate(*elim[:1], w_ref, v_ref, *elim[1:])
     g = dot_t(w_ref[...], dot(v_ref[...], fields_of(upper, 3)))
     out_ref[...] = table_ref[2 * R :, :] + dot_t(g, table_ref[R : 2 * R, :])
-    sent(started + first + second + third + fourth + fifth)
+    sent(started + first + second + list(third.values()) + fourth)
 
 
 def everything(scales, *operands):
@@ -455,9 +487,10 @@
         + sems
         + [
             pltpu.VMEM((3 * R + FIELDS, CHUNK), BF16),
-            pltpu.VMEM((R, 3 * R + FIELDS), F32),
-            pltpu.VMEM((R, 2 * R + FIELDS), F32),
-            pltpu.VMEM((R, R + FIELDS), F32),
+            pltpu.VMEM((3 * R + FIELDS, CHUNK), BF16),
+            pltpu.VMEM((FIELDS + R, R), F32),
+            pltpu.VMEM((FIELDS + 2 * R, R), F32),
+            pltpu.VMEM((FIELDS + 3 * R, R), F32),
             pltpu.VMEM((R, R), F32),
             pltpu.VMEM((R, R), F32),
             pltpu.VMEM((R, 2 * R + FIELDS), F32),

time: 101 us -> 85.7 us (0.85)
  Pallas kernels: 98.9 us -> 83.9 us
    pallas_call x1, Pallas kernels: 98.9 us -> 83.9 us  [everything(): pl.pallas_call(kernel, name='all', out_shape=shape(FIELDS, sites.shape[1]...]
where the time goes in v3:
time: 85.7 us; the launch traced here: 85.5 us
  Pallas kernels  83.9 us (98%)
  local copies, waits for them, and re-layouts  1.57 us (2%)
    pallas_call x1, Pallas kernels, everything(): pl.pallas_call(kernel, name='all', out_shape=shape(FIELDS, sites.shape[1]...  83.9 us

profile of v3, /device:TPU:1, one launch (start us, length us, event | category | flops | bytes accessed | tf_op | source)
XLA Modules:
  0.0 85.5 jit_solution(4733228274947255431)
XLA Ops:
  0.0 83.9 %all.1 = f32[64,512]{1,0:T(8,128)} custom-call(f32[3]{0:T(128)} %refs_0_.1, f32[2,256]{1,0:T(2,128)} %refs_1_.1, f32[2,256]{1,0:T(2,128)} %bitcast.8, f32[2,256]{1,0:T(2,128)} %bitcast.9, f32[2,4096]{1,0:T(2,128)} %refs_4_.1, f32[1,4096]{1,0:T(1,128)} %bitcast.7, bf16[64,4096]{1,0:T(8,128)(2,1)} %refs_6_.1, f32[2,512]{1,0:T(2,128)} %refs_7_.1, ...), custom_call_target="tpu_custom_call" | custom-call | tf_op jit(solution)/shard_map/all/pallas_call | solution.py:479
  83.9 1.6 %copy.13 = f32[64,512]{1,0:T(8,128)} copy(f32[64,512]{1,0:T(8,128)} %all.1) | data formatting | bytes 262144

commit v4 on v3

--- a/solution.py
+++ b/solution.py
@@ -61,7 +61,7 @@
     return jnp.concatenate([x, x], axis=1)
 
 
-def eliminate(f_ref, w_ref, v_ref, cols_ref, rows_ref, mine_ref, x_ref, lh_ref, xh_ref, hooks=()):
+def eliminate(f_ref, w_ref, d_ref, cols_ref, rows_ref, mine_ref, x_ref, lh_ref, xh_ref, hooks=()):
     lane = lax.broadcasted_iota(jnp.int32, (B, R), 1)
     sub = lax.broadcasted_iota(jnp.int32, (B, R), 0)
     sub_half = lax.broadcasted_iota(jnp.int32, (B, H), 0)
@@ -121,7 +121,7 @@
         x = twice(dcol) * mine
         done = lane < base + B
         w_ref[pl.ds(base, B), :] = jnp.where(done, mine, 0.0)
-        v_ref[pl.ds(base, B), :] = jnp.where(done, x, 0.0)
+        d_ref[pl.ds(base, B), :] = dcol
         mine_ref[...] = mine
         x_ref[...] = x
         lh_ref[...] = left_stack(jnp.where(done, 0.0, mine))
@@ -159,6 +159,12 @@
     return lax.dot_general(a, b, (((0,), (0,)), ((), ())), precision=HIGH, preferred_element_type=F32)
 
 
+def scaled(t, d_ref):
+    whole, rest = divmod(t.shape[1], H)
+    d = d_ref[...]
+    return t * jnp.concatenate([d] * whole + [d[:, :rest]] * (rest > 0), axis=1)
+
+
 def gram_of(a, b):
     return lax.dot_general(a, b, (((1,), (1,)), ((), ())), preferred_element_type=F32)
 
@@ -191,8 +197,30 @@
     out_ref[...] = jnp.concatenate(rows, axis=0).reshape(out_ref.shape)
 
 
-def whole_of(ref, first):
-    a, b, c = (ref[(first + n) * H : (first + n + 1) * H, :] for n in range(3))
+def pack_regional(out_ref, m):
+    q = H // 2
+    out_ref[0:H, :] = m[H:, :H]
+    out_ref[H : H + q, :] = m[q:H, :H]
+    out_ref[H + q : 2 * H, :] = m[H + q :, H:]
+    out_ref[2 * H : 2 * H + q, :] = jnp.concatenate([m[:q, :q], m[H : H + q, H : H + q]], axis=1)
+
+
+def regional_of(ref):
+    q = H // 2
+    corners = ref[2 * H : 2 * H + q, :]
+    blocks = [ref[0:H, :]]
+    for n in range(2):
+        low = ref[H + n * q : H + (n + 1) * q, :]
+        top = jnp.concatenate([corners[:, n * q : (n + 1) * q], low[:, :q].T], axis=1)
+        blocks.append(jnp.concatenate([top, low], axis=0))
+    b, a, c = blocks
+    return jnp.concatenate(
+        [jnp.concatenate([a, b.T], axis=1), jnp.concatenate([b, c], axis=1)], axis=0
+    )
+
+
+def whole_of(packed):
+    a, b, c = (packed[n * H : (n + 1) * H, :] for n in range(3))
     return jnp.concatenate(
         [jnp.concatenate([a, b.T], axis=1), jnp.concatenate([b, c], axis=1)], axis=0
     )
@@ -210,6 +238,7 @@
 NY, NX, NZ, NC = 8, 4, 8, 2
 GROUP = [(dx, dc) for dx in range(NX) for dc in range(NC)][1:]
 NEAREST = sorted(range(NY), key=lambda d: min(d, NY - d))
+FARTHEST = NEAREST[:0:-1]
 PLANE = [(dx, dy) for dy in NEAREST[::-1] for dx in range(NX) if (dx, dy) != (0, 0)]
 
 
@@ -280,7 +309,7 @@
     return [pltpu.SemaphoreType.DMA((count,)), pltpu.SemaphoreType.DMA((count,))]
 
 
-M_ROWS, C_ROWS = 3 * H, 5 * H
+M_ROWS, C_ROWS = 5 * H // 2, 5 * H
 M_PART, C_PART = M_ROWS // NY, C_ROWS // NY
 EXCHANGES = (7, 7, 7, 7, 7, 7, 7, 7, 31, 8)
 CROSS_STEP = 0
@@ -296,7 +325,7 @@
     (copy_sems,) = take(1)
     sems = [take(2) for _ in EXCHANGES]
     z_refs = take(2)
-    gv_ref, gr_ref, gg_ref, w_ref, v_ref, t2_ref, table_ref = take(7)
+    gv_ref, gr_ref, gg_ref, w_ref, d_ref, t2_ref, table_ref = take(7)
     mc_ref, gs_ref, m_ref, c_ref, m_in, c_in, g_in, g_sum, y_in = take(9)
     corr_ref, k_in, z_in, up_ref = take(4)
     elim = take(7)
@@ -345,11 +374,11 @@
     for copy in copies[6:]:
         copy.wait()
     f_ref[...] = prior_l[...] + gv_ref[FIELDS:, :]
-    eliminate(*elim[:1], w_ref, v_ref, *elim[1:])
+    eliminate(*elim[:1], w_ref, d_ref, *elim[1:])
 
     def scatter(rows, first, part, target, pair):
         copies = []
-        for d in range(1, NY):
+        for d in FARTHEST:
             place = on_y(d)
             at = pl.ds(pl.multiple_of(first + place[0] * part, 8), part)
             copies.append(send(rows.at[at, :], target.at[d - 1], pair, d - 1, place))
@@ -358,34 +387,32 @@
 
     def gather(ref, part, pair):
         at = pl.ds(pl.multiple_of(y * part, 8), part)
-        copies = [send(ref.at[at, :], ref.at[at, :], pair, d - 1, on_y(d)) for d in range(1, NY)]
+        copies = [send(ref.at[at, :], ref.at[at, :], pair, d - 1, on_y(d)) for d in FARTHEST]
         started.extend(copies)
         return copies
 
     leaf_rows = slice(FIELDS, FIELDS + R)
     region_rows = slice(FIELDS + R, FIELDS + 2 * R)
     t1 = dot(w_ref[...], gr_ref[leaf_rows, :])
-    t2_ref[:, :R] = dot(v_ref[...], gr_ref[leaf_rows, :])
+    t2_ref[:, :R] = scaled(t1, d_ref)
     regional = gr_ref[region_rows, :] - dot_t(t1, t2_ref[:, :R])
-    mc_ref[0:H, :] = regional[:H, :H]
-    mc_ref[H : 2 * H, :] = regional[H:, :H]
-    mc_ref[2 * H : 3 * H, :] = regional[H:, H:R]
+    pack_regional(mc_ref, regional)
     met()
     m_scatter = scatter(mc_ref, 0, M_PART, m_in, sems[0])
     right = jnp.concatenate([gg_ref[leaf_rows, :], gv_ref[:FIELDS, :].T], axis=1)
-    t2_ref[:, R:] = dot(v_ref[...], right)
+    t1_right = dot(w_ref[...], right)
+    t2_ref[:, R:] = scaled(t1_right, d_ref)
     regional = jnp.concatenate([gg_ref[region_rows, :], gr_ref[:FIELDS, :].T], axis=1) - dot_t(
         t1, t2_ref[:, R:]
     )
     for r in range(2):
         for n in range(2):
-            k = 3 + 2 * r + n
-            mc_ref[k * H : (k + 1) * H, :] = regional[r * H : (r + 1) * H, n * H : (n + 1) * H]
-    mc_ref[7 * H :, :] = jnp.concatenate([regional[:H, R:], regional[H:, R:]], axis=1)
+            k = M_ROWS + (2 * r + n) * H
+            mc_ref[k : k + H, :] = regional[r * H : (r + 1) * H, n * H : (n + 1) * H]
+    mc_ref[M_ROWS + 4 * H :, :] = jnp.concatenate([regional[:H, R:], regional[H:, R:]], axis=1)
     c_scatter = scatter(mc_ref, M_ROWS, C_PART, c_in, sems[3])
-    t1 = dot(w_ref[...], gg_ref[leaf_rows, :])
     upper = jnp.concatenate([gg_ref[FIELDS + 2 * R :, :], gg_ref[:FIELDS, :].T], axis=1)
-    pack_global(gs_ref, upper - dot_t(t1, t2_ref[:, R:]))
+    pack_global(gs_ref, upper - dot_t(t1_right[:, :R], t2_ref[:, R:]))
     g_scatter = []
     for n, d in enumerate(GROUP):
         place = on_xc(d)
@@ -404,7 +431,7 @@
     table_ref[2 * R :, :] = seen[2 * R :]
 
     arrived(m_gather)
-    f_ref[...] = prior_r[...] + whole_of(m_ref, 0)
+    f_ref[...] = prior_r[...] + regional_of(m_ref)
     later = {}
 
     def send_cross():
@@ -423,7 +450,7 @@
             later["y"].append(send(g_sum.at[place[0]], y_in.at[d - 1], sems[5], d - 1, place))
         started.extend(later["y"])
 
-    eliminate(*elim[:1], w_ref, v_ref, *elim[1:], hooks=[(CROSS_STEP, send_cross), (20, send_share)])
+    eliminate(*elim[:1], w_ref, d_ref, *elim[1:], hooks=[(CROSS_STEP, send_cross), (20, send_share)])
     arrived(later["c"])
     cross = jnp.concatenate(
         [
@@ -432,9 +459,9 @@
         ],
         axis=0,
     )
-    t1 = dot(w_ref[...], cross)
-    t2_ref[:, : R + FIELDS] = dot(v_ref[...], jnp.concatenate([cross, fields_of(c_ref, 4)], axis=1))
-    pack_global(corr_ref, dot_t(t1, t2_ref[:, : R + FIELDS]))
+    t1 = dot(w_ref[...], jnp.concatenate([cross, fields_of(c_ref, 4)], axis=1))
+    t2_ref[:, : R + FIELDS] = scaled(t1, d_ref)
+    pack_global(corr_ref, dot_t(t1[:, :R], t2_ref[:, : R + FIELDS]))
 
     first = []
     for n, d in enumerate(GROUP):
@@ -444,7 +471,7 @@
     share = added(g_sum[y], y_in)
     arrived(first)
     z_in[z] = share - added(corr_ref[c, y, x], k_in)
-    second = [send(z_in.at[z], z_in.at[z], sems[7], d - 1, on_z(d)) for d in range(1, NZ)]
+    second = [send(z_in.at[z], z_in.at[z], sems[7], d - 1, on_z(d)) for d in FARTHEST]
     sites_r = dot(w_ref[...], table_ref[:R, :])
     seen = dot_t(t2_ref[:, : R + FIELDS], sites_r)
     table_ref[R : 2 * R, :] -= seen[:R]
@@ -463,10 +490,11 @@
         fourth.append(send(block, block, sems[9], dy, on_xc((0, 1))))
     arrived(fourth)
     upper = up_ref[...].reshape(4 * H, H)
-    f_ref[...] = prior_g[...] + whole_of(upper, 0)
-    eliminate(*elim[:1], w_ref, v_ref, *elim[1:])
-    g = dot_t(w_ref[...], dot(v_ref[...], fields_of(upper, 3)))
-    out_ref[...] = table_ref[2 * R :, :] + dot_t(g, table_ref[R : 2 * R, :])
+    f_ref[...] = prior_g[...] + whole_of(upper)
+    eliminate(*elim[:1], w_ref, d_ref, *elim[1:])
+    nsite = table_ref.shape[1]
+    t1 = dot(w_ref[...], jnp.concatenate([table_ref[R : 2 * R, :], fields_of(upper, 3)], axis=1))
+    out_ref[...] = table_ref[2 * R :, :] + dot_t(scaled(t1[:, nsite:], d_ref), t1[:, :nsite])
     sent(started + first + second + list(third.values()) + fourth)
 
 
@@ -492,10 +520,10 @@
             pltpu.VMEM((FIELDS + 2 * R, R), F32),
             pltpu.VMEM((FIELDS + 3 * R, R), F32),
             pltpu.VMEM((R, R), F32),
-            pltpu.VMEM((R, R), F32),
+            pltpu.VMEM((R, H), F32),
             pltpu.VMEM((R, 2 * R + FIELDS), F32),
             pltpu.VMEM((2 * R + FIELDS, sites.shape[1]), F32),
-            pltpu.VMEM((8 * H, H), F32),
+            pltpu.VMEM((M_ROWS + C_ROWS, H), F32),
             tiles,
             pltpu.VMEM((M_ROWS, H), F32),
             pltpu.VMEM((C_ROWS, H), F32),

time: 85.7 us -> 83.1 us (0.970)
  Pallas kernels: 83.9 us -> 81.3 us
    pallas_call x1, Pallas kernels: 83.9 us -> 81.3 us  [everything(): pl.pallas_call(kernel, name='all', out_shape=shape(FIELDS, sites.shape[1]...]
where the time goes in v4:
time: 83.1 us; the launch traced here: 82.9 us
  Pallas kernels  81.3 us (98%)
  local copies, waits for them, and re-layouts  1.57 us (2%)
    pallas_call x1, Pallas kernels, everything(): pl.pallas_call(kernel, name='all', out_shape=shape(FIELDS, sites.shape[1]...  81.3 us

profile of v4, /device:TPU:1, one launch (start us, length us, event | category | flops | bytes accessed | tf_op | source)
XLA Modules:
  0.0 82.9 jit_solution(11776419531988577627)
XLA Ops:
  0.0 81.3 %all.1 = f32[64,512]{1,0:T(8,128)} custom-call(f32[3]{0:T(128)} %refs_0_.1, f32[2,256]{1,0:T(2,128)} %refs_1_.1, f32[2,256]{1,0:T(2,128)} %bitcast.8, f32[2,256]{1,0:T(2,128)} %bitcast.9, f32[2,4096]{1,0:T(2,128)} %refs_4_.1, f32[1,4096]{1,0:T(1,128)} %bitcast.7, bf16[64,4096]{1,0:T(8,128)(2,1)} %refs_6_.1, f32[2,512]{1,0:T(2,128)} %refs_7_.1, ...), custom_call_target="tpu_custom_call" | custom-call | tf_op jit(solution)/shard_map/all/pallas_call | solution.py:507
  81.3 1.6 %copy.13 = f32[64,512]{1,0:T(8,128)} copy(f32[64,512]{1,0:T(8,128)} %all.1) | data formatting | bytes 262144

commit v5 on v4

--- a/solution.py
+++ b/solution.py
@@ -312,7 +312,6 @@
 M_ROWS, C_ROWS = 5 * H // 2, 5 * H
 M_PART, C_PART = M_ROWS // NY, C_ROWS // NY
 EXCHANGES = (7, 7, 7, 7, 7, 7, 7, 7, 31, 8)
-CROSS_STEP = 0
 
 
 def kernel(*refs):
@@ -430,8 +429,6 @@
     table_ref[R : 2 * R, :] = basis(knots[2], places, scales[2]) - seen[R : 2 * R]
     table_ref[2 * R :, :] = seen[2 * R :]
 
-    arrived(m_gather)
-    f_ref[...] = prior_r[...] + regional_of(m_ref)
     later = {}
 
     def send_cross():
@@ -450,7 +447,10 @@
             later["y"].append(send(g_sum.at[place[0]], y_in.at[d - 1], sems[5], d - 1, place))
         started.extend(later["y"])
 
-    eliminate(*elim[:1], w_ref, d_ref, *elim[1:], hooks=[(CROSS_STEP, send_cross), (20, send_share)])
+    send_cross()
+    arrived(m_gather)
+    f_ref[...] = prior_r[...] + regional_of(m_ref)
+    eliminate(*elim[:1], w_ref, d_ref, *elim[1:], hooks=[(20, send_share)])
     arrived(later["c"])
     cross = jnp.concatenate(
         [

time: 83.1 us -> 82.7 us (level)
  no operation moved by 1% of the time
where the time goes in v5:
time: 82.7 us; the launch traced here: 82.5 us
  Pallas kernels  81 us (98%)
  local copies, waits for them, and re-layouts  1.57 us (2%)
    pallas_call x1, Pallas kernels, everything(): pl.pallas_call(kernel, name='all', out_shape=shape(FIELDS, sites.shape[1]...  81 us

profile of v5, /device:TPU:1, one launch (start us, length us, event | category | flops | bytes accessed | tf_op | source)
XLA Modules:
  0.0 82.5 jit_solution(2516948027647625361)
XLA Ops:
  0.0 81.0 %all.1 = f32[64,512]{1,0:T(8,128)} custom-call(f32[3]{0:T(128)} %refs_0_.1, f32[2,256]{1,0:T(2,128)} %refs_1_.1, f32[2,256]{1,0:T(2,128)} %bitcast.8, f32[2,256]{1,0:T(2,128)} %bitcast.9, f32[2,4096]{1,0:T(2,128)} %refs_4_.1, f32[1,4096]{1,0:T(1,128)} %bitcast.7, bf16[64,4096]{1,0:T(8,128)(2,1)} %refs_6_.1, f32[2,512]{1,0:T(2,128)} %refs_7_.1, ...), custom_call_target="tpu_custom_call" | custom-call | tf_op jit(solution)/shard_map/all/pallas_call | solution.py:507
  81.0 1.6 %copy.13 = f32[64,512]{1,0:T(8,128)} copy(f32[64,512]{1,0:T(8,128)} %all.1) | data formatting | bytes 262144
